TPU v7x, 32 devices: a whole 2x2x4 slice. The times are simulated.
32 devices in a mesh: grp: 2 (over y), res: 8 (over z, x), ta: 2 (over core).
Axes of the slice: x: 2, y: 2, z: 4, core: 2. Of those that a mesh axis runs over, the one named last changes fastest.
Arguments:
- log_order: int32 [8, 512], P('res'), may hold values from 1 to 4096, as said below
- t_start: int32 [2], P('grp'), parts along dimension 0, may hold values from 160 to 319
- term_counts: int32 [1024], P(('grp', 'ta')), parts along dimension 0, may hold values from 4 to 32, as said below
Outputs:
- refined: float32 [2, 8, 512, 2048], P(None, None, 'res', ('grp', 'ta')), parts along dimension 3
There are 2 independent parts, one for each index of `grp`. A program takes and returns all parts, laid end to end along the dimension named above; an argument that names none is the same for every part. Nothing has to cross between parts.
Inputs may be any that keep to these rules, and one draw needn't show every extreme that they name: `log_order`: every residue 1 to 4096 appears once. `term_counts`: at least an eighth of t_m plus two, except at the first point.
All inputs are finite; a program needn't handle non-finite values.
Results may differ from a plain program's by a relative error of at most 0.00023.
Values sent between devices are 32-bit elements; how exact they have to be, the bound alone decides.
A program may use at most 64 MiB of HBM per device.

v0:
```python
import math

import jax
import jax.numpy as jnp
from jax import lax
from jax.sharding import PartitionSpec as P

TAPS = 8
MAXN = 32


time_step = 0.0625


def padded_2(block, sides, width):
    for axis, dim in sides:
        count = lax.axis_size(axis)
        forward = [(i, i + 1) for i in range(count - 1)]
        backward = [(target, source) for source, target in forward]
        low = lax.ppermute(
            lax.slice_in_dim(block, block.shape[dim] - width, None, axis=dim), axis, forward
        )
        high = lax.ppermute(lax.slice_in_dim(block, 0, width, axis=dim), axis, backward)
        block = jnp.concatenate([low, block, high], axis=dim)
    return block


def inverse_power(base_value, t_values):
    modulus = lax.rsqrt(base_value)
    phase_now = t_values * jnp.log(base_value)
    return (modulus * jnp.cos(phase_now), -modulus * jnp.sin(phase_now))


def hurwitz_values(x_values, t_values, count_row, most_terms):
    shape_out = (x_values.shape[0], t_values.shape[1])

    def add_term(term_index, running):
        sum_re, sum_im = running
        base_value = term_index.astype(x_values.dtype) + x_values
        piece_re, piece_im = inverse_power(base_value, t_values)
        active = term_index < count_row
        return (
            sum_re + jnp.where(active, piece_re, 0.0),
            sum_im + jnp.where(active, piece_im, 0.0),
        )

    zeros_init = jnp.zeros(shape_out, x_values.dtype)
    sum_re, sum_im = lax.fori_loop(0, most_terms, add_term, (zeros_init, zeros_init))
    tail_base = count_row.astype(x_values.dtype) + x_values
    power_re, power_im = inverse_power(tail_base, t_values)
    denominator = 0.25 + t_values * t_values
    lifted_re = tail_base * power_re
    lifted_im = tail_base * power_im
    total_re = sum_re + (-0.5 * lifted_re + t_values * lifted_im) / denominator + 0.5 * power_re
    total_im = sum_im + (-t_values * lifted_re - 0.5 * lifted_im) / denominator + 0.5 * power_im
    total_re = total_re + (0.5 * power_re - t_values * power_im) / (12.0 * tail_base)
    total_im = total_im + (0.5 * power_im + t_values * power_re) / (12.0 * tail_base)
    cubic_re = 1.875 - 4.5 * t_values * t_values
    cubic_im = 5.75 * t_values - t_values * t_values * t_values
    cube_base = 720.0 * tail_base * tail_base * tail_base
    total_re = total_re - (cubic_re * power_re - cubic_im * power_im) / cube_base
    total_im = total_im - (cubic_re * power_im + cubic_im * power_re) / cube_base
    return (total_re, total_im)


def sinc_value(offset):
    return math.sin(math.pi * offset) / (math.pi * offset)


def refine(padded, half_width, length):
    coarse = padded[..., half_width : half_width + length]
    middle = jnp.zeros_like(coarse)
    for offset in range(1 - half_width, half_width + 1):
        weight = sinc_value(offset - 0.5) * sinc_value((offset - 0.5) / half_width)
        middle = middle + weight * padded[..., half_width + offset : half_width + offset + length]
    stacked = jnp.stack([coarse, middle], axis=-1)
    return stacked.reshape(stacked.shape[:-2] + (2 * length,))


def matmul_high(left, right):
    return jnp.dot(left, right, precision=lax.Precision.HIGHEST, preferred_element_type=jnp.float32)


def per_device(log_order, t_start, term_counts):
    rows_here = log_order.shape[1]
    slabs = lax.axis_size("res")
    slab_index = lax.axis_index("res")
    length_here = term_counts.shape[0]
    ta_index = lax.axis_index("ta")
    modulus_int = slabs * rows_here + 1
    x_values = log_order.reshape(rows_here, 1).astype(jnp.float32) / jnp.float32(modulus_int)
    row_ids = jnp.arange(rows_here, dtype=jnp.int32)
    first_phase = (row_ids[:, None] * row_ids[None, :] % rows_here).astype(jnp.float32) * (
        2.0 * math.pi / rows_here
    )
    first_cos = jnp.cos(first_phase)
    first_sin = jnp.sin(first_phase)
    twist_phase = (row_ids * slab_index).astype(jnp.float32)[:, None] * (
        2.0 * math.pi / (slabs * rows_here)
    )
    twist_cos = jnp.cos(twist_phase)
    twist_sin = jnp.sin(twist_phase)
    slab_ids = jnp.arange(slabs, dtype=jnp.int32)
    second_phase = (slab_ids[:, None] * slab_ids[None, :] % slabs).astype(jnp.float32) * (
        2.0 * math.pi / slabs
    )
    second_cos = jnp.cos(second_phase)
    second_sin = jnp.sin(second_phase)
    positions = ta_index * length_here + jnp.arange(length_here, dtype=jnp.int32)
    count_row = term_counts[None, :]
    t_values = ((t_start[0] + positions).astype(jnp.float32) * time_step)[None, :]
    zeta_re, zeta_im = hurwitz_values(x_values, t_values, count_row, MAXN)
    mixed_re = matmul_high(first_cos, zeta_re) - matmul_high(first_sin, zeta_im)
    mixed_im = matmul_high(first_sin, zeta_re) + matmul_high(first_cos, zeta_im)
    turned_re = twist_cos * mixed_re - twist_sin * mixed_im
    turned_im = twist_sin * mixed_re + twist_cos * mixed_im
    sectioned = jnp.stack([turned_re, turned_im])[:, None]
    block_in = lax.all_to_all(sectioned, "res", split_axis=2, concat_axis=1, tiled=True)
    part_re = block_in[0]
    part_im = block_in[1]

    def mix(table, values):
        return jnp.einsum(
            "wp,psn->wsn",
            table,
            values,
            precision=lax.Precision.HIGHEST,
            preferred_element_type=jnp.float32,
        )

    out_re = mix(second_cos, part_re) - mix(second_sin, part_im)
    out_im = mix(second_sin, part_re) + mix(second_cos, part_im)
    spectrum = jnp.stack([out_re, out_im])
    factor_re, factor_im = inverse_power(jnp.float32(modulus_int), t_values)
    lval_re = spectrum[0] * factor_re - spectrum[1] * factor_im
    lval_im = spectrum[0] * factor_im + spectrum[1] * factor_re
    lvals = jnp.stack([lval_re, lval_im])
    padded = padded_2(lvals, (("ta", 3),), TAPS)
    return refine(padded, TAPS, length_here)


def solution(mesh):
    placed = (P("res", None), P("grp"), P(("grp", "ta")))
    return jax.shard_map(
        per_device,
        mesh=mesh,
        in_specs=placed,
        out_specs=P(None, None, "res", ("grp", "ta")),
        check_vma=False,
    )
```

profile of v0, /device:TPU:0, one launch (start us, length us, event | category | flops | bytes accessed | tf_op | source)
XLA Modules:
  0.0 207.3 jit_solution(16231159181828599554)
XLA Ops:
  2.1 121.0 %while.16 = (s32[]{:T(128)}, f32[512,256]{1,0:T(8,128)S(1)}, f32[512,256]{1,0:T(8,128)S(1)}, s32[1,256]{1,0:T(1,128)}, f32[512,1]{0,1:T(1,128)S(1)}, /*index=5*/s32[]{:T(128)}, s32[]{:T(128)}, s32[]{:T(128)}, s32[]{:T(128)}) while((s32[]{:T(128)}, f32[512,256]{1,0:T(8,128)S(1)}, f32[512,256]{1,0:T(8,128)S(1)}, s32[1,256]{1,0:T(1,128)}, ...), condition=%wide.region_1.2_spmd.clone, body=%wide.region_0.1_spmd.clone.sunk | while | flops 1181956 | bytes 2117255 | solution.py:48
  3.4 2.4 %fusion.139 = (f32[512,256]{1,0:T(8,128)S(1)}, f32[512,256]{1,0:T(8,128)S(1)}) fusion(f32[512,256]{1,0:T(8,128)S(1)} %get-tuple-element.249, f32[512]{0:T(512)S(1)} %neg.53, f32[512]{0:T(512)S(1)} %bitcast.58, f32[256]{0:T(256)S(1)} %bitcast.59, pred[]{:T(512)S(6)} %compare.5, pred[256]{0:T(512)(128)(4,1)S(1)} %compare_reduce_fusion.2, ...), kind=kLoop, calls=%fused_computation.8.clone.1 | loop fusion | flops 1179648 | bytes 2104577 | tf_op jit(solution)/shard_map/while/body/eval_jaxpr/add | solution.py:44
  7.2 2.4 %fusion.139 = (f32[512,256]{1,0:T(8,128)S(1)}, f32[512,256]{1,0:T(8,128)S(1)}) fusion(f32[512,256]{1,0:T(8,128)S(1)} %get-tuple-element.249, f32[512]{0:T(512)S(1)} %neg.53, f32[512]{0:T(512)S(1)} %bitcast.58, f32[256]{0:T(256)S(1)} %bitcast.59, pred[]{:T(512)S(6)} %compare.5, pred[256]{0:T(512)(128)(4,1)S(1)} %compare_reduce_fusion.2, ...), kind=kLoop, calls=%fused_computation.8.clone.1 | loop fusion | flops 1179648 | bytes 2104577 | tf_op jit(solution)/shard_map/while/body/eval_jaxpr/add | solution.py:44
  14.8 2.4 %fusion.139 = (f32[512,256]{1,0:T(8,128)S(1)}, f32[512,256]{1,0:T(8,128)S(1)}) fusion(f32[512,256]{1,0:T(8,128)S(1)} %get-tuple-element.249, f32[512]{0:T(512)S(1)} %neg.53, f32[512]{0:T(512)S(1)} %bitcast.58, f32[256]{0:T(256)S(1)} %bitcast.59, pred[]{:T(512)S(6)} %compare.5, pred[256]{0:T(512)(128)(4,1)S(1)} %compare_reduce_fusion.2, ...), kind=kLoop, calls=%fused_computation.8.clone.1 | loop fusion | flops 1179648 | bytes 2104577 | tf_op jit(solution)/shard_map/while/body/eval_jaxpr/add | solution.py:44
  18.6 2.4 %fusion.139 = (f32[512,256]{1,0:T(8,128)S(1)}, f32[512,256]{1,0:T(8,128)S(1)}) fusion(f32[512,256]{1,0:T(8,128)S(1)} %get-tuple-element.249, f32[512]{0:T(512)S(1)} %neg.53, f32[512]{0:T(512)S(1)} %bitcast.58, f32[256]{0:T(256)S(1)} %bitcast.59, pred[]{:T(512)S(6)} %compare.5, pred[256]{0:T(512)(128)(4,1)S(1)} %compare_reduce_fusion.2, ...), kind=kLoop, calls=%fused_computation.8.clone.1 | loop fusion | flops 1179648 | bytes 2104577 | tf_op jit(solution)/shard_map/while/body/eval_jaxpr/add | solution.py:44
  22.4 2.4 %fusion.139 = (f32[512,256]{1,0:T(8,128)S(1)}, f32[512,256]{1,0:T(8,128)S(1)}) fusion(f32[512,256]{1,0:T(8,128)S(1)} %get-tuple-element.249, f32[512]{0:T(512)S(1)} %neg.53, f32[512]{0:T(512)S(1)} %bitcast.58, f32[256]{0:T(256)S(1)} %bitcast.59, pred[]{:T(512)S(6)} %compare.5, pred[256]{0:T(512)(128)(4,1)S(1)} %compare_reduce_fusion.2, ...), kind=kLoop, calls=%fused_computation.8.clone.1 | loop fusion | flops 1179648 | bytes 2104577 | tf_op jit(solution)/shard_map/while/body/eval_jaxpr/add | solution.py:44
  26.1 2.4 %fusion.139 = (f32[512,256]{1,0:T(8,128)S(1)}, f32[512,256]{1,0:T(8,128)S(1)}) fusion(f32[512,256]{1,0:T(8,128)S(1)} %get-tuple-element.249, f32[512]{0:T(512)S(1)} %neg.53, f32[512]{0:T(512)S(1)} %bitcast.58, f32[256]{0:T(256)S(1)} %bitcast.59, pred[]{:T(512)S(6)} %compare.5, pred[256]{0:T(512)(128)(4,1)S(1)} %compare_reduce_fusion.2, ...), kind=kLoop, calls=%fused_computation.8.clone.1 | loop fusion | flops 1179648 | bytes 2104577 | tf_op jit(solution)/shard_map/while/body/eval_jaxpr/add | solution.py:44
  29.9 2.4 %fusion.139 = (f32[512,256]{1,0:T(8,128)S(1)}, f32[512,256]{1,0:T(8,128)S(1)}) fusion(f32[512,256]{1,0:T(8,128)S(1)} %get-tuple-element.249, f32[512]{0:T(512)S(1)} %neg.53, f32[512]{0:T(512)S(1)} %bitcast.58, f32[256]{0:T(256)S(1)} %bitcast.59, pred[]{:T(512)S(6)} %compare.5, pred[256]{0:T(512)(128)(4,1)S(1)} %compare_reduce_fusion.2, ...), kind=kLoop, calls=%fused_computation.8.clone.1 | loop fusion | flops 1179648 | bytes 2104577 | tf_op jit(solution)/shard_map/while/body/eval_jaxpr/add | solution.py:44
  33.7 2.4 %fusion.139 = (f32[512,256]{1,0:T(8,128)S(1)}, f32[512,256]{1,0:T(8,128)S(1)}) fusion(f32[512,256]{1,0:T(8,128)S(1)} %get-tuple-element.249, f32[512]{0:T(512)S(1)} %neg.53, f32[512]{0:T(512)S(1)} %bitcast.58, f32[256]{0:T(256)S(1)} %bitcast.59, pred[]{:T(512)S(6)} %compare.5, pred[256]{0:T(512)(128)(4,1)S(1)} %compare_reduce_fusion.2, ...), kind=kLoop, calls=%fused_computation.8.clone.1 | loop fusion | flops 1179648 | bytes 2104577 | tf_op jit(solution)/shard_map/while/body/eval_jaxpr/add | solution.py:44
  41.3 2.4 %fusion.139 = (f32[512,256]{1,0:T(8,128)S(1)}, f32[512,256]{1,0:T(8,128)S(1)}) fusion(f32[512,256]{1,0:T(8,128)S(1)} %get-tuple-element.249, f32[512]{0:T(512)S(1)} %neg.53, f32[512]{0:T(512)S(1)} %bitcast.58, f32[256]{0:T(256)S(1)} %bitcast.59, pred[]{:T(512)S(6)} %compare.5, pred[256]{0:T(512)(128)(4,1)S(1)} %compare_reduce_fusion.2, ...), kind=kLoop, calls=%fused_computation.8.clone.1 | loop fusion | flops 1179648 | bytes 2104577 | tf_op jit(solution)/shard_map/while/body/eval_jaxpr/add | solution.py:44
  45.1 2.4 %fusion.139 = (f32[512,256]{1,0:T(8,128)S(1)}, f32[512,256]{1,0:T(8,128)S(1)}) fusion(f32[512,256]{1,0:T(8,128)S(1)} %get-tuple-element.249, f32[512]{0:T(512)S(1)} %neg.53, f32[512]{0:T(512)S(1)} %bitcast.58, f32[256]{0:T(256)S(1)} %bitcast.59, pred[]{:T(512)S(6)} %compare.5, pred[256]{0:T(512)(128)(4,1)S(1)} %compare_reduce_fusion.2, ...), kind=kLoop, calls=%fused_computation.8.clone.1 | loop fusion | flops 1179648 | bytes 2104577 | tf_op jit(solution)/shard_map/while/body/eval_jaxpr/add | solution.py:44
  48.8 2.4 %fusion.139 = (f32[512,256]{1,0:T(8,128)S(1)}, f32[512,256]{1,0:T(8,128)S(1)}) fusion(f32[512,256]{1,0:T(8,128)S(1)} %get-tuple-element.249, f32[512]{0:T(512)S(1)} %neg.53, f32[512]{0:T(512)S(1)} %bitcast.58, f32[256]{0:T(256)S(1)} %bitcast.59, pred[]{:T(512)S(6)} %compare.5, pred[256]{0:T(512)(128)(4,1)S(1)} %compare_reduce_fusion.2, ...), kind=kLoop, calls=%fused_computation.8.clone.1 | loop fusion | flops 1179648 | bytes 2104577 | tf_op jit(solution)/shard_map/while/body/eval_jaxpr/add | solution.py:44
  52.6 2.4 %fusion.139 = (f32[512,256]{1,0:T(8,128)S(1)}, f32[512,256]{1,0:T(8,128)S(1)}) fusion(f32[512,256]{1,0:T(8,128)S(1)} %get-tuple-element.249, f32[512]{0:T(512)S(1)} %neg.53, f32[512]{0:T(512)S(1)} %bitcast.58, f32[256]{0:T(256)S(1)} %bitcast.59, pred[]{:T(512)S(6)} %compare.5, pred[256]{0:T(512)(128)(4,1)S(1)} %compare_reduce_fusion.2, ...), kind=kLoop, calls=%fused_computation.8.clone.1 | loop fusion | flops 1179648 | bytes 2104577 | tf_op jit(solution)/shard_map/while/body/eval_jaxpr/add | solution.py:44
  56.4 2.4 %fusion.139 = (f32[512,256]{1,0:T(8,128)S(1)}, f32[512,256]{1,0:T(8,128)S(1)}) fusion(f32[512,256]{1,0:T(8,128)S(1)} %get-tuple-element.249, f32[512]{0:T(512)S(1)} %neg.53, f32[512]{0:T(512)S(1)} %bitcast.58, f32[256]{0:T(256)S(1)} %bitcast.59, pred[]{:T(512)S(6)} %compare.5, pred[256]{0:T(512)(128)(4,1)S(1)} %compare_reduce_fusion.2, ...), kind=kLoop, calls=%fused_computation.8.clone.1 | loop fusion | flops 1179648 | bytes 2104577 | tf_op jit(solution)/shard_map/while/body/eval_jaxpr/add | solution.py:44
  123.1 2.9 %fusion.38 = (f32[512,256]{1,0:T(8,128)S(1)}, f32[512,256]{1,0:T(8,128)S(1)}) fusion(f32[512,256]{1,0:T(8,128)S(1)} %get-tuple-element.116, f32[256]{0:T(256)S(1)} %fusion.93, f32[256]{0:T(256)S(1)} %get-tuple-element.180, f32[256]{0:T(256)S(1)} %get-tuple-element.183, f32[256]{0:T(256)S(1)} %get-tuple-element.179, f32[256]{0:T(256)S(1)} %get-tuple-element.184, ...), kind=kLoop, calls=%fused_computation.82 | loop fusion | flops 5636096 | bytes 2105344 | tf_op jit(solution)/shard_map/sub | solution.py:62
  126.0 5.6 %fusion.65 = f32[512,256]{1,0:T(8,128)S(1)} fusion(f32[512,256]{1,0:T(8,128)S(1)} %get-tuple-element.176), kind=kOutput, calls=%fused_computation.111 | convolution fusion | flops 808976384 | bytes 1048576 | tf_op jit(solution)/shard_map/dot_general | solution.py:81
  131.6 5.6 %fusion.63 = f32[512,256]{1,0:T(8,128)S(1)} fusion(f32[512,256]{1,0:T(8,128)S(1)} %get-tuple-element.176), kind=kOutput, calls=%fused_computation.110 | convolution fusion | flops 808976384 | bytes 1048576 | tf_op jit(solution)/shard_map/dot_general | solution.py:81
  137.3 5.6 %convolution_add_fusion = f32[512,256]{1,0:T(8,128)S(1)} fusion(f32[512,256]{1,0:T(8,128)S(1)} %fusion.65, f32[512,256]{1,0:T(8,128)S(1)} %get-tuple-element.175), kind=kOutput, calls=%fused_computation.32 | convolution fusion | flops 809107456 | bytes 1572864 | tf_op jit(solution)/shard_map/dot_general | solution.py:81
  142.9 7.2 %subtract_bitcast_fusion.1 = (f32[1,512,256]{2,1,0:T(8,128)S(1)}, f32[1,512,256]{2,1,0:T(8,128)S(1)}) fusion(f32[512,256]{1,0:T(8,128)S(1)} %convolution_add_fusion, f32[512]{0:T(512)S(1)} %get-tuple-element.185, f32[512]{0:T(512)S(1)} %get-tuple-element.186, f32[512,256]{1,0:T(8,128)S(1)} %fusion.63, f32[512,256]{1,0:T(8,128)S(1)} %get-tuple-element.175), kind=kOutput, calls=%fused_computation.107 | convolution fusion | flops 809893888 | bytes 2625536 | tf_op jit(solution)/shard_map/dot_general | solution.py:81
  152.0 7.3 %all-to-all-start = ((f32[2,1,512,256]{3,0,1,2:T(2,128)}), f32[2,1,512,256]{3,0,1,2:T(2,128)S(1)}, u32[]{:S(2)}, u32[]{:S(2)}) async-start(f32[2,1,512,256]{3,0,1,2:T(2,128)} %copy.17), calls=%async_computation | async-start | bytes 2097152 | tf_op jit(solution)/shard_map/all_to_all | solution.py:118
  159.3 25.7 %all-to-all-done = f32[2,1,512,256]{3,0,1,2:T(2,128)S(1)} async-done(((f32[2,1,512,256]{3,0,1,2:T(2,128)}), f32[2,1,512,256]{3,0,1,2:T(2,128)S(1)}, u32[]{:S(2)}, u32[]{:S(2)}) %all-to-all-start) | async-done | bytes 1048608 | tf_op jit(solution)/shard_map/all_to_all | solution.py:118
  195.2 4.2 %fusion.30 = (f32[2,8,64,256,1]{3,1,2,0,4:T(8,128)S(1)}, f32[2,8,64,256,1]{3,1,2,0,4:T(8,128)S(1)}) fusion(f32[1,8,64,256]{3,1,2,0:T(8,128)S(1)} %get-tuple-element.165, f32[1,8,64,256]{3,1,2,0:T(8,128)S(1)} %get-tuple-element.166, f32[2,8,64,264]{3,1,2,0:T(8,128)S(1)} %get-tuple-element.170, f32[2,8,64,264]{3,1,2,0:T(8,128)S(1)} %get-tuple-element.169), kind=kLoop, calls=%fused_computation.74 | loop fusion | flops 8388608 | bytes 18874368 | tf_op jit(solution)/shard_map/stack | solution.py:76
  199.6 3.9 %copy.24 = f32[2,8,64,256,2]{2,1,4,3,0:T(8,128)} copy(f32[2,8,64,256,2]{3,1,2,0,4:T(8,128)S(1)} %pad_maximum_fusion) | data formatting | bytes 4194304 | tf_op jit(solution)/shard_map/stack | solution.py:76
  203.5 3.8 %copy.25 = f32[2,8,64,512]{3,2,1,0:T(8,128)} copy(f32[2,8,64,512]{2,1,3,0:T(8,128)} %bitcast.51) | data formatting | bytes 4194304 | tf_op jit(solution)/shard_map/reshape | solution.py:77
  (172 shorter events, 102.5 us)
Async XLA Ops:
  152.0 33.0 %all-to-all-start = ((f32[2,1,512,256]{3,0,1,2:T(2,128)}), f32[2,1,512,256]{3,0,1,2:T(2,128)S(1)}, u32[]{:S(2)}, u32[]{:S(2)}) async-start(f32[2,1,512,256]{3,0,1,2:T(2,128)} %copy.17), calls=%async_computation | async-start | bytes 2097152 | tf_op jit(solution)/shard_map/all_to_all | solution.py:118
  189.6 2.8 %collective-permute-start = (f32[2,8,64,8]{3,1,2,0:T(8,128)S(1)}, f32[2,8,64,8]{3,1,2,0:T(8,128)S(1)}, u32[]{:S(2)}, u32[]{:S(2)}) collective-permute-start(f32[2,8,64,8]{3,1,2,0:T(8,128)S(1)} %get-tuple-element.171), channel_id=1, source_target_pairs={{0,1},{2,3},{4,5},{6,7},{8,9},{10,11},{12,13},{14,15},{16,17},{18,... | collective-permute-start | bytes 98312 | tf_op jit(solution)/shard_map/ppermute | solution.py:20
  190.9 3.8 %collective-permute-start.1 = (f32[2,8,64,8]{3,1,2,0:T(8,128)S(1)}, f32[2,8,64,8]{3,1,2,0:T(8,128)S(1)}, u32[]{:S(2)}, u32[]{:S(2)}) collective-permute-start(f32[2,8,64,8]{3,1,2,0:T(8,128)S(1)} %get-tuple-element.172), channel_id=1, source_target_pairs={{1,0},{3,2},{5,4},{7,6},{9,8},{11,10},{13,12},{15,14},{17,16},{19,... | collective-permute-start | bytes 98312 | tf_op jit(solution)/shard_map/ppermute | solution.py:23
where the time goes:
time: 210 us; the launch traced here: 207 us
  other arithmetic  129 us (61%)
  waiting for transfers between devices  28.2 us (13%)
  matrix products  27.5 us (13%)
  local copies, waits for them, and re-layouts  10.4 us (5%)
  starting transfers between devices  9.87 us (5%)
    add x32, other arithmetic, add_term(): sum_im + jnp.where(active, piece_im, 0.0)  75.7 us
    all_to_all x1, waiting for transfers between devices, per_device(): lax.all_to_all(sectioned, 'res', split_axis=2, concat_axis=1, tiled=True)  25.7 us
    dot_general x4, matrix products, matmul_high(): jnp.dot(left, right, precision=lax.Precision.HIGHEST, preferred_element_t...  24.1 us
    lt x32, other arithmetic, add_term(): active = term_index < count_row  22.4 us
    mul x32, other arithmetic, per_device(): (t_start[0] + positions).astype(jnp.float32) * time_step  20.9 us
    all_to_all x1, starting transfers between devices, per_device(): lax.all_to_all(sectioned, 'res', split_axis=2, concat_axis=1, tiled=True)  7.26 us
    another operation x2, other arithmetic, refine(): stacked = jnp.stack([coarse, middle], axis=-1)  4.36 us
  transfers between devices with their start and end apart: 3, of which 3 were waited for; matrix products, arithmetic and copies ran while one was open for 0% of the time, Pallas kernels for 0%

commit v1 on v0

--- a/solution.py
+++ b/solution.py
@@ -1,12 +1,413 @@
+import functools
 import math
 
 import jax
 import jax.numpy as jnp
+import ml_dtypes
+import numpy as np
 from jax import lax
+from jax.experimental import pallas as pl
+from jax.experimental.pallas import tpu as pltpu
 from jax.sharding import PartitionSpec as P
 
 TAPS = 8
 MAXN = 32
+LANES = 128
+TILE = 8
+
+SIN_COEFS = (
+    6.2831854820251465, -41.34170150756836, 81.60513305664062, -76.7030029296875,
+    42.02585220336914, -14.899578094482422, 3.2377800941467285,
+)
+COS_COEFS = (
+    1.0, -19.73920440673828, 64.93911743164062, -85.45011138916016,
+    60.16743087768555, -25.96688461303711, 6.527706146240234,
+)
+ROUNDER = 12582912.0
+
+
+def sincos_turns(turns):
+    frac = turns - ((turns + ROUNDER) - ROUNDER)
+    square = frac * frac
+    sin_acc = jnp.full_like(square, SIN_COEFS[-1])
+    cos_acc = jnp.full_like(square, COS_COEFS[-1])
+    for sin_c, cos_c in zip(SIN_COEFS[-2::-1], COS_COEFS[-2::-1]):
+        sin_acc = sin_acc * square + sin_c
+        cos_acc = cos_acc * square + cos_c
+    return sin_acc * frac, cos_acc
+
+
+def split_bf16(values):
+    high = values.astype(jnp.bfloat16)
+    return high, (values - high.astype(jnp.float32)).astype(jnp.bfloat16)
+
+
+def split_const(values):
+    high = values.astype(np.float32).astype(ml_dtypes.bfloat16)
+    low = (values - high.astype(np.float64)).astype(np.float32).astype(ml_dtypes.bfloat16)
+    return high, low
+
+
+def dot_nt(left, right):
+    return lax.dot_general(
+        left, right, (((1,), (1,)), ((), ())), preferred_element_type=jnp.float32
+    )
+
+
+def dot_nn(left, right):
+    return jnp.dot(left, right, preferred_element_type=jnp.float32)
+
+
+def fourier_table(rows):
+    ids = np.arange(rows)
+    phase = 2.0 * np.pi * (np.outer(ids, ids) % rows) / rows
+    return np.stack(split_const(np.cos(phase)) + split_const(np.sin(phase)))
+
+
+def sinc_value(offset):
+    return math.sin(math.pi * offset) / (math.pi * offset)
+
+
+def tap_weight(offset):
+    return sinc_value(offset - 0.5) * sinc_value((offset - 0.5) / TAPS)
+
+
+def refine_table(length):
+    table = np.zeros((length, 2 * length))
+    for m in range(length):
+        table[m, 2 * m] = 1.0
+        for offset in range(1 - TAPS, TAPS + 1):
+            if 0 <= m + offset < length:
+                table[m + offset, 2 * m + 1] = tap_weight(offset)
+    return np.stack(split_const(table))
+
+
+def edge_table(length, slabs):
+    side = np.zeros((2, TILE, LANES))
+    for h in range(TAPS):
+        for column in range(LANES):
+            if column % 2 == 0:
+                continue
+            m = (2 * length - LANES + column) // 2
+            offset = length + h - m
+            if 1 - TAPS <= offset <= TAPS:
+                side[0, h, column] = tap_weight(offset)
+            m = column // 2
+            offset = h - TAPS - m
+            if 1 - TAPS <= offset <= TAPS:
+                side[1, h, column] = tap_weight(offset)
+    full = np.zeros((2, slabs * TILE, slabs * LANES))
+    for slab in range(slabs):
+        full[:, slab * TILE : (slab + 1) * TILE, slab * LANES : (slab + 1) * LANES] = side
+    high, low = split_const(full)
+    return np.stack([high, low], axis=1)
+
+
+class Shape:
+    def __init__(self, rows, slabs, length):
+        self.rows = rows
+        self.slabs = slabs
+        self.length = length
+        self.block = rows // slabs
+        self.tiles = length // TILE + 1
+        self.halves = length // LANES
+
+
+def prepare(shape, order_ref, turn_re, turn_im, wave_re, wave_im, base_t):
+    rows = shape.rows
+    modulus = float(shape.slabs * rows + 1)
+    order_row = order_ref[...].astype(jnp.float32)
+    term = lax.broadcasted_iota(jnp.int32, (MAXN, rows), 0).astype(jnp.float32)
+    base = term * modulus + order_row
+    log_turn = jnp.log(base) * (1.0 / (2.0 * math.pi))
+    amp = lax.rsqrt(base)
+    step_sin, step_cos = sincos_turns(log_turn * (TILE / 16.0))
+    offsets = lax.broadcasted_iota(jnp.int32, (TILE, rows), 0).astype(jnp.float32)
+    t_first = (base_t + offsets) * 0.0625
+    for n in range(MAXN):
+        sin, cos = sincos_turns(t_first * log_turn[n : n + 1, :])
+        amp_row = amp[n : n + 1, :]
+        wave_re[n] = amp_row * cos
+        wave_im[n] = -amp_row * sin
+        turn_re[n] = jnp.broadcast_to(step_cos[n : n + 1, :], (TILE, rows))
+        turn_im[n] = jnp.broadcast_to(-step_sin[n : n + 1, :], (TILE, rows))
+
+
+def sum_tiles(shape, first, count, order_ref, counts, turn_re, turn_im, wave_re, wave_im, zeta_re, zeta_im, base_t):
+    modulus = float(shape.slabs * shape.rows + 1)
+    row0 = first * TILE
+
+    def lane_block(block, carry):
+        lanes = pl.ds(pl.multiple_of(block * LANES, LANES), LANES)
+        limits = [counts[row0 + a * TILE : row0 + (a + 1) * TILE, :] for a in range(count)]
+
+        def term(n, sums):
+            now_re = wave_re[n, :, lanes]
+            now_im = wave_im[n, :, lanes]
+            rot_re = turn_re[n, :, lanes]
+            rot_im = turn_im[n, :, lanes]
+            n_float = lax.convert_element_type(n, jnp.float32)
+            out = []
+            for a in range(count):
+                active = limits[a] > n_float
+                out.append(sums[2 * a] + jnp.where(active, now_re, 0.0))
+                out.append(sums[2 * a + 1] + jnp.where(active, now_im, 0.0))
+                now_re, now_im = (
+                    now_re * rot_re - now_im * rot_im,
+                    now_re * rot_im + now_im * rot_re,
+                )
+            wave_re[n, :, lanes] = now_re
+            wave_im[n, :, lanes] = now_im
+            return tuple(out)
+
+        zero = jnp.zeros((TILE, LANES), jnp.float32)
+        sums = lax.fori_loop(0, MAXN, term, (zero,) * (2 * count))
+        residue = jnp.broadcast_to(order_ref[:, lanes].astype(jnp.float32), (TILE, LANES))
+        fraction = residue * (1.0 / modulus)
+        offsets = lax.broadcasted_iota(jnp.int32, (TILE, LANES), 0).astype(jnp.float32)
+        for a in range(count):
+            limit = limits[a]
+            t_now = (base_t + float(row0 + a * TILE) + offsets) * 0.0625
+            t_square = t_now * t_now
+            inverse_den = 1.0 / (0.25 + t_square)
+            cubic_re = 1.875 - 4.5 * t_square
+            cubic_im = t_now * (5.75 - t_square)
+            whole_base = limit * modulus + residue
+            tail_base = limit + fraction
+            inverse = 1.0 / tail_base
+            cube = inverse * inverse * inverse * (1.0 / 720.0)
+            twelfth = inverse * (1.0 / 12.0)
+            lifted = tail_base * inverse_den
+            gain_re = 0.5 + 0.5 * twelfth - 0.5 * lifted - cubic_re * cube
+            gain_im = t_now * (twelfth - lifted) - cubic_im * cube
+            sin, cos = sincos_turns(t_now * (jnp.log(whole_base) * (1.0 / (2.0 * math.pi))))
+            amp = lax.rsqrt(whole_base)
+            power_re = amp * cos
+            power_im = -amp * sin
+            place = slice(row0 + a * TILE, row0 + (a + 1) * TILE)
+            zeta_re[place, lanes] = sums[2 * a] + (gain_re * power_re - gain_im * power_im)
+            zeta_im[place, lanes] = sums[2 * a + 1] + (gain_re * power_im + gain_im * power_re)
+        return carry
+
+    lax.fori_loop(0, shape.rows // LANES, lane_block, 0)
+
+
+def make_twist(shape, slab_index, twist_cos, twist_sin):
+    ids = lax.broadcasted_iota(jnp.int32, (shape.rows, LANES), 0)
+    turns = (ids * slab_index).astype(jnp.float32) * (1.0 / (shape.slabs * shape.rows))
+    sin, cos = sincos_turns(turns)
+    twist_cos[...] = cos
+    twist_sin[...] = sin
+
+
+def transform_half(shape, half, skip, zeta_re, zeta_im, tables, twist_cos, twist_sin, store):
+    place = pl.ds(pl.multiple_of(half * LANES + skip, TILE), LANES)
+    both = jnp.concatenate([zeta_re[place, :], zeta_im[place, :]], axis=0)
+    high, low = split_bf16(both)
+    chunk = 2 * shape.block
+    for piece in range(shape.rows // chunk):
+        rows = slice(piece * chunk, (piece + 1) * chunk)
+        cos_high = tables[0, rows, :]
+        sin_high = tables[2, rows, :]
+        with_cos = dot_nt(cos_high, high) + dot_nt(cos_high, low) + dot_nt(tables[1, rows, :], high)
+        with_sin = dot_nt(sin_high, high) + dot_nt(sin_high, low) + dot_nt(tables[3, rows, :], high)
+        mixed_re = with_cos[:, :LANES] - with_sin[:, LANES:]
+        mixed_im = with_sin[:, :LANES] + with_cos[:, LANES:]
+        t_cos = twist_cos[rows, :]
+        t_sin = twist_sin[rows, :]
+        out_re = t_cos * mixed_re - t_sin * mixed_im
+        out_im = t_sin * mixed_re + t_cos * mixed_im
+        for sub in range(2):
+            cut = slice(sub * shape.block, (sub + 1) * shape.block)
+            store(2 * piece + sub, 0, out_re[cut])
+            store(2 * piece + sub, 1, out_im[cut])
+
+
+def transform_edge(shape, place, slab_index, zeta_re, zeta_im, tables, store):
+    both = jnp.concatenate([zeta_re[place, :], zeta_im[place, :]], axis=0)
+    high, low = split_bf16(both)
+    with_cos = dot_nn(high, tables[0]) + dot_nn(low, tables[0]) + dot_nn(high, tables[1])
+    with_sin = dot_nn(high, tables[2]) + dot_nn(low, tables[2]) + dot_nn(high, tables[3])
+    mixed_re = with_cos[:TILE] - with_sin[TILE:]
+    mixed_im = with_sin[:TILE] + with_cos[TILE:]
+    ids = lax.broadcasted_iota(jnp.int32, (TILE, shape.rows), 1)
+    sin, cos = sincos_turns(
+        (ids * slab_index).astype(jnp.float32) * (1.0 / (shape.slabs * shape.rows))
+    )
+    out_re = cos * mixed_re - sin * mixed_im
+    out_im = sin * mixed_re + cos * mixed_im
+    lane = lax.broadcasted_iota(jnp.int32, (TILE, LANES), 1)
+    for pair in range(shape.slabs // 2):
+        cut = slice(pair * LANES, (pair + 1) * LANES)
+        part_re = out_re[:, cut]
+        part_im = out_im[:, cut]
+        store(2 * pair, jnp.where(lane < LANES // 2, part_re, pltpu.roll(part_im, LANES // 2, 1)))
+        store(
+            2 * pair + 1,
+            jnp.where(lane < LANES // 2, pltpu.roll(part_re, LANES // 2, 1), part_im),
+        )
+
+
+def column_counts(shape, counts_row, counts):
+    width = counts.shape[0]
+    row = jnp.broadcast_to(counts_row.astype(jnp.float32), (LANES, width))
+    for cut in range(width // LANES):
+        part = row[:, cut * LANES : (cut + 1) * LANES]
+        counts[cut * LANES : (cut + 1) * LANES, :] = part.T
+
+
+def zeta_kernel(shape, start_ref, order_ref, count_ref, tables, main_ref, edge_ref,
+                turn_re, turn_im, wave_re, wave_im, zeta_re, zeta_im, counts, twist_cos, twist_sin):
+    slab_index = lax.axis_index("res")
+    ta_index = lax.axis_index("ta")
+    skip = ta_index * TILE
+    base_t = (start_ref[0] + ta_index * (shape.length - TILE)).astype(jnp.float32)
+    column_counts(shape, count_ref[...], counts)
+    make_twist(shape, slab_index, twist_cos, twist_sin)
+    prepare(shape, order_ref, turn_re, turn_im, wave_re, wave_im, base_t)
+    first = 0
+    for half in range(shape.halves):
+        for count in ((9, 8) if half == 0 else (8, 8)):
+            sum_tiles(shape, first, count, order_ref, counts, turn_re, turn_im, wave_re, wave_im,
+                      zeta_re, zeta_im, base_t)
+            first += count
+
+        def store(block, part, values, half=half):
+            main_ref[half, block, part] = values
+
+        transform_half(shape, half, skip, zeta_re, zeta_im, tables, twist_cos, twist_sin, store)
+
+    def store_edge(block, values):
+        edge_ref[block] = values
+
+    edge_place = pl.ds(pl.multiple_of((1 - ta_index) * shape.length, TILE), TILE)
+    transform_edge(shape, edge_place, slab_index, zeta_re, zeta_im, tables, store_edge)
+
+
+def turn_eighth(re, im, eighths):
+    root = math.sqrt(0.5)
+    if eighths == 0:
+        return re, im
+    if eighths == 1:
+        return root * (re - im), root * (re + im)
+    if eighths == 2:
+        return -im, re
+    return -root * (re + im), root * (re - im)
+
+
+def fft_eight(parts):
+    def step(values):
+        size = len(values)
+        if size == 1:
+            return values
+        even = step(values[0::2])
+        odd = step(values[1::2])
+        low, high = [], []
+        for k in range(size // 2):
+            o_re, o_im = turn_eighth(*odd[k], k * (8 // size))
+            e_re, e_im = even[k]
+            low.append((e_re + o_re, e_im + o_im))
+            high.append((e_re - o_re, e_im - o_im))
+        return low + high
+
+    return step(parts)
+
+
+def refine_kernel(shape, chunk, main_ref, edge_ref, table, edge_tab, out_ref, edge_out):
+    step = pl.program_id(0)
+    slabs = shape.slabs
+    half_lanes = LANES // 2
+    ta_index = lax.axis_index("ta")
+
+    @pl.when(step == 0)
+    def _():
+        lane = lax.broadcasted_iota(jnp.int32, (TILE, LANES), 1)
+        parts = [(edge_ref[p], pltpu.roll(edge_ref[p], half_lanes, 1)) for p in range(slabs)]
+        mixed = fft_eight(parts)
+        rows = [jnp.where(lane < half_lanes, re, pltpu.roll(im, half_lanes, 1)) for re, im in mixed]
+        stacked = jnp.concatenate(rows + rows, axis=0)
+        high, low = split_bf16(stacked.T[:, : slabs * TILE])
+        tab_high = edge_tab[ta_index, 0]
+        tab_low = edge_tab[ta_index, 1]
+        edge_out[...] = dot_nn(high, tab_high) + dot_nn(low, tab_high) + dot_nn(high, tab_low)
+
+    parts = []
+    for p in range(slabs):
+        re = jnp.concatenate([main_ref[h, p, 0] for h in range(shape.halves)], axis=1)
+        im = jnp.concatenate([main_ref[h, p, 1] for h in range(shape.halves)], axis=1)
+        parts.append((re, im))
+    mixed = fft_eight(parts)
+    stacked = jnp.concatenate([m[0] for m in mixed] + [m[1] for m in mixed], axis=0)
+    high, low = split_bf16(stacked)
+    result = dot_nn(high, table[0]) + dot_nn(low, table[0]) + dot_nn(high, table[1])
+    edge_lanes = pl.ds(
+        pl.multiple_of((1 - ta_index) * (2 * shape.length - LANES), LANES), LANES
+    )
+    for part in range(2):
+        rows = pl.ds(pl.multiple_of(part * shape.block + step * chunk, TILE), chunk)
+        for w in range(slabs):
+            at = (part * slabs + w) * chunk
+            out_ref[part, w] = result[at : at + chunk]
+            out_ref[part, w, :, edge_lanes] += edge_out[rows, w * LANES : (w + 1) * LANES]
+
+
+def fast_device(log_order, t_start, term_counts):
+    shape = Shape(log_order.shape[1], lax.axis_size("res"), term_counts.shape[0])
+    rows, slabs, length = shape.rows, shape.slabs, shape.length
+    ta_index = lax.axis_index("ta")
+    other = lax.ppermute(term_counts, "ta", [(0, 1), (1, 0)])
+    pad = jnp.full((LANES - TILE,), MAXN, jnp.int32)
+    counts = jnp.where(
+        ta_index == 0,
+        jnp.concatenate([term_counts, other[:TILE], pad]),
+        jnp.concatenate([other[length - TILE :], term_counts, pad]),
+    )
+    f32 = jnp.float32
+    vmem = pl.BlockSpec(memory_space=pltpu.VMEM)
+    main, edge = pl.pallas_call(
+        functools.partial(zeta_kernel, shape),
+        out_shape=(
+            jax.ShapeDtypeStruct((shape.halves, slabs, 2, shape.block, LANES), f32),
+            jax.ShapeDtypeStruct((slabs, TILE, LANES), f32),
+        ),
+        in_specs=[pl.BlockSpec(memory_space=pltpu.SMEM), vmem, vmem, vmem],
+        out_specs=(vmem, vmem),
+        scratch_shapes=[
+            pltpu.VMEM((MAXN, TILE, rows), f32),
+            pltpu.VMEM((MAXN, TILE, rows), f32),
+            pltpu.VMEM((MAXN, TILE, rows), f32),
+            pltpu.VMEM((MAXN, TILE, rows), f32),
+            pltpu.VMEM((length + TILE, rows), f32),
+            pltpu.VMEM((length + TILE, rows), f32),
+            pltpu.VMEM((length + LANES, LANES), f32),
+            pltpu.VMEM((rows, LANES), f32),
+            pltpu.VMEM((rows, LANES), f32),
+        ],
+        compiler_params=pltpu.CompilerParams(vmem_limit_bytes=48 * 2**20),
+    )(t_start, log_order, counts[None, :], jnp.asarray(fourier_table(rows)))
+    main = lax.all_to_all(main, "res", split_axis=1, concat_axis=1, tiled=True)
+    edge = lax.all_to_all(edge, "res", split_axis=0, concat_axis=0, tiled=True)
+    return refine_call(shape, main, edge)
+
+
+def refine_call(shape, main, edge):
+    slabs, length = shape.slabs, shape.length
+    chunk = 16
+    f32 = jnp.float32
+    return pl.pallas_call(
+        functools.partial(refine_kernel, shape, chunk),
+        grid=(shape.block // chunk,),
+        out_shape=jax.ShapeDtypeStruct((2, slabs, shape.block, 2 * length), f32),
+        in_specs=[
+            pl.BlockSpec((shape.halves, slabs, 2, chunk, LANES), lambda i: (0, 0, 0, i, 0)),
+            pl.BlockSpec((slabs, TILE, LANES), lambda i: (0, 0, 0)),
+            pl.BlockSpec((2, length, 2 * length), lambda i: (0, 0, 0)),
+            pl.BlockSpec((2, 2, slabs * TILE, slabs * LANES), lambda i: (0, 0, 0, 0)),
+        ],
+        out_specs=pl.BlockSpec((2, slabs, chunk, 2 * length), lambda i: (0, 0, i, 0)),
+        scratch_shapes=[pltpu.VMEM((LANES, slabs * LANES), f32)],
+        compiler_params=pltpu.CompilerParams(vmem_limit_bytes=48 * 2**20),
+    )(main, edge, jnp.asarray(refine_table(length)), jnp.asarray(edge_table(length, slabs)))
 
 
 time_step = 0.0625
@@ -63,10 +464,6 @@
     return (total_re, total_im)
 
 
-def sinc_value(offset):
-    return math.sin(math.pi * offset) / (math.pi * offset)
-
-
 def refine(padded, half_width, length):
     coarse = padded[..., half_width : half_width + length]
     middle = jnp.zeros_like(coarse)
@@ -142,7 +539,7 @@
 def solution(mesh):
     placed = (P("res", None), P("grp"), P(("grp", "ta")))
     return jax.shard_map(
-        per_device,
+        fast_device if mesh.shape["res"] == 8 and mesh.shape["ta"] == 2 else per_device,
         mesh=mesh,
         in_specs=placed,
         out_specs=P(None, None, "res", ("grp", "ta")),

time: 210 us -> 72.4 us (0.34); the launches traced: 207 us -> 72 us
  other arithmetic: 129 us -> 0.83 us
  blocking collectives: 0 us -> 33.1 us
  matrix products: 27.5 us -> 0 us
  Pallas kernels: 0 us -> 23.8 us
  waiting for transfers between devices: 28.2 us -> 6.87 us
  local copies, waits for them, and re-layouts: 10.4 us -> 2.63 us
  starting transfers between devices: 9.87 us -> 4.09 us
    add x33 -> x0, other arithmetic: 75.7 us -> none  [the longest x32 75.7 us: add_term(): sum_im + jnp.where(active, piece_im, 0.0)]
    all_to_all x0 -> x1, blocking collectives: none -> 33.1 us  [fast_device(): main = lax.all_to_all(main, 'res', split_axis=1, concat_axis=1, tiled=True)]
    dot_general x8 -> x0, matrix products: 27.5 us -> none  [the longest x4 24.1 us: matmul_high(): jnp.dot(left, right, precision=lax.Precision.HIGHEST, preferred_element_t...]
    pallas_call x0 -> x2, Pallas kernels: none -> 23.8 us  [the longest x1 20.3 us: fast_device(): pl.pallas_call(functools.partial(zeta_kernel, shape), out_shape=(jax.Shap...]
    lt x32 -> x0, other arithmetic: 22.4 us -> none  [add_term(): active = term_index < count_row]
    mul x33 -> x0, other arithmetic: 20.9 us -> none  [the longest x32 20.9 us: per_device(): (t_start[0] + positions).astype(jnp.float32) * time_step]
    all_to_all x1, waiting for transfers between devices: 25.7 us -> 6.58 us  [fast_device(): edge = lax.all_to_all(edge, 'res', split_axis=0, concat_axis=0, tiled=True)]
    another operation x3 -> x0, other arithmetic: 4.56 us -> none  [the longest x2 4.36 us: refine(): stacked = jnp.stack([coarse, middle], axis=-1)]
  transfers between devices with their start and end apart: 3 -> 2, of which waited for: 3 -> 2; matrix products, arithmetic and copies ran while one was open for 0% -> 0% of each run, Pallas kernels for 0% -> 0%
where the time goes in v1:
time: 72.4 us; the launch traced here: 72 us
  blocking collectives  33.1 us (46%)
  Pallas kernels  23.8 us (33%)
  waiting for transfers between devices  6.87 us (9%)
  starting transfers between devices  4.09 us (6%)
  local copies, waits for them, and re-layouts  2.63 us (4%)
  other arithmetic  0.83 us (1%)
    all_to_all x1, blocking collectives, fast_device(): main = lax.all_to_all(main, 'res', split_axis=1, concat_axis=1, tiled=True)  33.1 us
    pallas_call x1, Pallas kernels, fast_device(): pl.pallas_call(functools.partial(zeta_kernel, shape), out_shape=(jax.Shap...  20.3 us
    all_to_all x1, waiting for transfers between devices, fast_device(): edge = lax.all_to_all(edge, 'res', split_axis=0, concat_axis=0, tiled=True)  6.58 us
    all_to_all x1, starting transfers between devices, fast_device(): edge = lax.all_to_all(edge, 'res', split_axis=0, concat_axis=0, tiled=True)  3.64 us
    pallas_call x1, Pallas kernels, refine_call(): pl.pallas_call(functools.partial(refine_kernel, shape, chunk), grid=(shap...  3.5 us
    unnamed x8, local copies, waits for them, and re-layouts  2.29 us
  transfers between devices with their start and end apart: 2, of which 2 were waited for; matrix products, arithmetic and copies ran while one was open for 0% of the time, Pallas kernels for 0%

profile of v1, /device:TPU:0, one launch (start us, length us, event | category | flops | bytes accessed | tf_op | source)
XLA Modules:
  0.0 72.0 jit_solution(14174733576523352748)
XLA Ops:
  0.0 0.5 collective-permute-start
  1.1 0.1 pad.5.clone
  1.2 0.3 collective-permute-done
  1.5 0.1 slice_bitcast_fusion
  1.6 0.8 %broadcast_select_fusion.count_ref = s32[1,384]{1,0:T(1,128)S(1)} fusion(pred[]{:T(512)S(6)} %eq.3, s32[1,8]{1,0:T(1,128)S(1)} %get-tuple-element.10, s32[1,256]{1,0:T(1,128)} %bitcast.5, s32[384]{0:T(512)S(1)} %pad.5.clone, s32[1,8]{1,0:T(1,128)S(1)} %get-tuple-element.9), kind=kLoop, calls=%fused_computation | loop fusion | flops 1920 | bytes 4161 | tf_op jit(solution)/shard_map/jit(_where)/select_n | solution.py:360
  2.4 0.0 copy-start
  2.4 1.6 %copy-done = bf16[4,512,512]{2,1,0:T(8,128)(2,1)S(1)} copy-done((bf16[4,512,512]{2,1,0:T(8,128)(2,1)S(1)}, bf16[4,512,512]{2,1,0:T(8,128)(2,1)}, u32[]{:S(2)}) %copy-start) | copy-done | bytes 2097176
  4.0 0.0 copy-start.3
  4.0 0.7 copy-done.3
  4.7 20.3 %shard_map.64 = (f32[2,8,2,64,128]{4,3,2,1,0:T(8,128)S(1)}, f32[8,8,128]{2,1,0:T(8,128)}) custom-call(s32[1]{0:T(128)S(6)} %copy.9.start_ref, s32[1,512]{1,0:T(1,128)S(1)} %copy-done.3, s32[1,384]{1,0:T(1,128)S(1)} %broadcast_select_fusion.count_ref, bf16[4,512,512]{2,1,0:T(8,128)(2,1)S(1)} %copy-done), custom_call_target="tpu_custom_call" | custom-call | tf_op jit(solution)/shard_map/pallas_call | solution.py:367
  25.0 0.1 copy.7
  25.1 0.0 copy-start.1
  25.1 0.0 copy-start.2
  25.1 33.1 %all_to_all.10 = f32[2,8,2,64,128]{4,3,2,0,1:T(8,128)S(1)} all-to-all(f32[2,8,2,64,128]{4,3,2,0,1:T(8,128)S(1)} %copy.7), channel_id=1, replica_groups=mesh['grp'=2,'res'=8,'ta'=2] {'res'}, dimensions={1} | all-to-all | bytes 2097152 | tf_op jit(solution)/shard_map/all_to_all | solution.py:388
  58.2 3.6 %all-to-all-start.1 = ((f32[8,8,128]{2,1,0:T(8,128)}), f32[8,8,128]{2,1,0:T(8,128)S(1)}, u32[]{:S(2)}, u32[]{:S(2)}) async-start(f32[8,8,128]{2,1,0:T(8,128)} %get-tuple-element.8), calls=%async_computation.1 | async-start | bytes 65536 | tf_op jit(solution)/shard_map/all_to_all | solution.py:389
  61.9 0.1 copy.8.main_ref
  62.0 6.6 %all-to-all-done.1.edge_ref = f32[8,8,128]{2,1,0:T(8,128)S(1)} async-done(((f32[8,8,128]{2,1,0:T(8,128)}), f32[8,8,128]{2,1,0:T(8,128)S(1)}, u32[]{:S(2)}, u32[]{:S(2)}) %all-to-all-start.1) | async-done | bytes 32800 | tf_op jit(solution)/shard_map/all_to_all | solution.py:389
  68.5 0.0 copy-done.1
  68.5 0.0 copy-done.2
  68.5 3.5 %shard_map.65 = f32[2,8,64,512]{3,2,1,0:T(8,128)} custom-call(f32[2,8,2,64,128]{4,3,2,1,0:T(8,128)S(1)} %copy.8.main_ref, f32[8,8,128]{2,1,0:T(8,128)S(1)} %all-to-all-done.1.edge_ref, bf16[2,256,512]{2,1,0:T(8,128)(2,1)S(1)} %copy-done.2, bf16[2,2,64,1024]{3,2,1,0:T(8,128)(2,1)S(1)} %copy-done.1), custom_call_target="tpu_custom_call" | custom-call | tf_op jit(solution)/shard_map/pallas_call | solution.py:397
  (1 shorter events, 0.0 us)
Async XLA Ops:
  0.0 1.5 %collective-permute-start = (s32[256]{0:T(256)}, s32[256]{0:T(256)S(1)}, u32[]{:S(2)}, u32[]{:S(2)}) collective-permute-start(s32[256]{0:T(256)} %param.8), channel_id=1, source_target_pairs={{0,1},{1,0},{2,3},{3,2},{4,5},{5,4},{6,7},{7,6},{8,9},{9,8},{10,11... | collective-permute-start | bytes 3080 | tf_op jit(solution)/shard_map/ppermute | solution.py:358
  2.4 1.6 %copy-start = (bf16[4,512,512]{2,1,0:T(8,128)(2,1)S(1)}, bf16[4,512,512]{2,1,0:T(8,128)(2,1)}, u32[]{:S(2)}) copy-start(bf16[4,512,512]{2,1,0:T(8,128)(2,1)} %constant.14.clone.tables) | copy-start | bytes 6291460
  4.0 0.7 copy-start.3
  25.1 43.5 %copy-start.1 = (bf16[2,2,64,1024]{3,2,1,0:T(8,128)(2,1)S(1)}, bf16[2,2,64,1024]{3,2,1,0:T(8,128)(2,1)}, u32[]{:S(2)}) copy-start(bf16[2,2,64,1024]{3,2,1,0:T(8,128)(2,1)} %constant.16.clone.edge_tab) | copy-start | bytes 1572868
  25.1 43.5 %copy-start.2 = (bf16[2,256,512]{2,1,0:T(8,128)(2,1)S(1)}, bf16[2,256,512]{2,1,0:T(8,128)(2,1)}, u32[]{:S(2)}) copy-start(bf16[2,256,512]{2,1,0:T(8,128)(2,1)} %constant.15.clone.table) | copy-start | bytes 1572868
  58.2 10.3 %all-to-all-start.1 = ((f32[8,8,128]{2,1,0:T(8,128)}), f32[8,8,128]{2,1,0:T(8,128)S(1)}, u32[]{:S(2)}, u32[]{:S(2)}) async-start(f32[8,8,128]{2,1,0:T(8,128)} %get-tuple-element.8), calls=%async_computation.1 | async-start | bytes 65536 | tf_op jit(solution)/shard_map/all_to_all | solution.py:389

commit v2 on v1

--- a/solution.py
+++ b/solution.py
@@ -161,7 +161,7 @@
             return tuple(out)
 
         zero = jnp.zeros((TILE, LANES), jnp.float32)
-        sums = lax.fori_loop(0, MAXN, term, (zero,) * (2 * count))
+        sums = lax.fori_loop(0, MAXN, term, (zero,) * (2 * count), unroll=4)
         residue = jnp.broadcast_to(order_ref[:, lanes].astype(jnp.float32), (TILE, LANES))
         fraction = residue * (1.0 / modulus)
         offsets = lax.broadcasted_iota(jnp.int32, (TILE, LANES), 0).astype(jnp.float32)
@@ -248,40 +248,88 @@
         )
 
 
-def column_counts(shape, counts_row, counts):
-    width = counts.shape[0]
-    row = jnp.broadcast_to(counts_row.astype(jnp.float32), (LANES, width))
-    for cut in range(width // LANES):
-        part = row[:, cut * LANES : (cut + 1) * LANES]
-        counts[cut * LANES : (cut + 1) * LANES, :] = part.T
-
-
-def zeta_kernel(shape, start_ref, order_ref, count_ref, tables, main_ref, edge_ref,
-                turn_re, turn_im, wave_re, wave_im, zeta_re, zeta_im, counts, twist_cos, twist_sin):
-    slab_index = lax.axis_index("res")
+def column_counts(shape, own_row, other_row, own_at, other_from, other_at, counts, spare):
+    def columns(row_ref, cut):
+        lanes = slice(cut * LANES, (cut + 1) * LANES)
+        return jnp.broadcast_to(row_ref[:, lanes].astype(jnp.float32), (LANES, LANES)).T
+
+    for cut in range(shape.halves):
+        at = pl.ds(pl.multiple_of(own_at + cut * LANES, TILE), LANES)
+        counts[at, :] = columns(own_row, cut)
+        spare[cut * LANES : (cut + 1) * LANES, :] = columns(other_row, cut)
+    counts[pl.ds(pl.multiple_of(other_at, TILE), TILE), :] = spare[
+        pl.ds(pl.multiple_of(other_from, TILE), TILE), :
+    ]
+
+
+def zeta_kernel(shape, start_ref, order_ref, count_ref, table_hbm, main_out, edge_out, main_send, edge_send,
+                other_counts, spare, tables, turn_re, turn_im, wave_re, wave_im, zeta_re, zeta_im, counts,
+                twist_cos, twist_sin, table_sem, count_sems, main_send_sems, main_recv_sems,
+                edge_send_sems, edge_recv_sems):
+    slabs, length = shape.slabs, shape.length
+    me = lax.axis_index("res")
     ta_index = lax.axis_index("ta")
-    skip = ta_index * TILE
-    base_t = (start_ref[0] + ta_index * (shape.length - TILE)).astype(jnp.float32)
-    column_counts(shape, count_ref[...], counts)
-    make_twist(shape, slab_index, twist_cos, twist_sin)
+    mesh_ids = pl.DeviceIdType.MESH
+    peers = [lax.rem(me + d, slabs) for d in range(slabs)]
+
+    barrier = pltpu.get_barrier_semaphore()
+    for d in range(1, slabs):
+        pl.semaphore_signal(barrier, inc=1, device_id={"res": peers[d]}, device_id_type=mesh_ids)
+    pl.semaphore_signal(barrier, inc=1, device_id={"ta": 1 - ta_index}, device_id_type=mesh_ids)
+    table_copy = pltpu.make_async_copy(table_hbm, tables, table_sem)
+    table_copy.start()
+
+    base_t = (start_ref[0] + ta_index * (length - TILE)).astype(jnp.float32)
+    make_twist(shape, me, twist_cos, twist_sin)
+    pl.semaphore_wait(barrier, slabs)
+    count_copy = pltpu.make_async_remote_copy(
+        src_ref=count_ref, dst_ref=other_counts, send_sem=count_sems.at[0], recv_sem=count_sems.at[1],
+        device_id={"ta": 1 - ta_index}, device_id_type=mesh_ids,
+    )
+    count_copy.start()
     prepare(shape, order_ref, turn_re, turn_im, wave_re, wave_im, base_t)
+    count_copy.wait()
+    column_counts(shape, count_ref, other_counts, ta_index * TILE, ta_index * (length - TILE),
+                  (1 - ta_index) * length, counts, spare)
+
+    copies = []
+
+    def send(source, target, send_sems, recv_sems, d):
+        copy = pltpu.make_async_remote_copy(
+            src_ref=source, dst_ref=target, send_sem=send_sems, recv_sem=recv_sems,
+            device_id={"res": peers[d]}, device_id_type=mesh_ids,
+        )
+        copy.start()
+        copies.append(copy)
+
     first = 0
     for half in range(shape.halves):
         for count in ((9, 8) if half == 0 else (8, 8)):
             sum_tiles(shape, first, count, order_ref, counts, turn_re, turn_im, wave_re, wave_im,
                       zeta_re, zeta_im, base_t)
             first += count
+        if half == 0:
+            table_copy.wait()
 
         def store(block, part, values, half=half):
-            main_ref[half, block, part] = values
-
-        transform_half(shape, half, skip, zeta_re, zeta_im, tables, twist_cos, twist_sin, store)
+            main_send[half, block, part] = values
+
+        transform_half(shape, half, ta_index * TILE, zeta_re, zeta_im, tables, twist_cos, twist_sin, store)
+        for d in range(1, slabs):
+            send(main_send.at[half, peers[d]], main_out.at[half, me],
+                 main_send_sems.at[half, d], main_recv_sems.at[half, d], d)
+        main_out[half, me] = main_send[half, me]
 
     def store_edge(block, values):
-        edge_ref[block] = values
-
-    edge_place = pl.ds(pl.multiple_of((1 - ta_index) * shape.length, TILE), TILE)
-    transform_edge(shape, edge_place, slab_index, zeta_re, zeta_im, tables, store_edge)
+        edge_send[block] = values
+
+    edge_place = pl.ds(pl.multiple_of((1 - ta_index) * length, TILE), TILE)
+    transform_edge(shape, edge_place, me, zeta_re, zeta_im, tables, store_edge)
+    for d in range(1, slabs):
+        send(edge_send.at[peers[d]], edge_out.at[me], edge_send_sems.at[d], edge_recv_sems.at[d], d)
+    edge_out[me] = edge_send[me]
+    for copy in copies:
+        copy.wait()
 
 
 def turn_eighth(re, im, eighths):
@@ -354,39 +402,42 @@
 def fast_device(log_order, t_start, term_counts):
     shape = Shape(log_order.shape[1], lax.axis_size("res"), term_counts.shape[0])
     rows, slabs, length = shape.rows, shape.slabs, shape.length
-    ta_index = lax.axis_index("ta")
-    other = lax.ppermute(term_counts, "ta", [(0, 1), (1, 0)])
-    pad = jnp.full((LANES - TILE,), MAXN, jnp.int32)
-    counts = jnp.where(
-        ta_index == 0,
-        jnp.concatenate([term_counts, other[:TILE], pad]),
-        jnp.concatenate([other[length - TILE :], term_counts, pad]),
-    )
     f32 = jnp.float32
     vmem = pl.BlockSpec(memory_space=pltpu.VMEM)
+    main_shape = (shape.halves, slabs, 2, shape.block, LANES)
+    edge_shape = (slabs, TILE, LANES)
+    table = fourier_table(rows)
     main, edge = pl.pallas_call(
         functools.partial(zeta_kernel, shape),
-        out_shape=(
-            jax.ShapeDtypeStruct((shape.halves, slabs, 2, shape.block, LANES), f32),
-            jax.ShapeDtypeStruct((slabs, TILE, LANES), f32),
-        ),
-        in_specs=[pl.BlockSpec(memory_space=pltpu.SMEM), vmem, vmem, vmem],
+        out_shape=(jax.ShapeDtypeStruct(main_shape, f32), jax.ShapeDtypeStruct(edge_shape, f32)),
+        in_specs=[pl.BlockSpec(memory_space=pltpu.SMEM), vmem, vmem, pl.BlockSpec(memory_space=pltpu.HBM)],
         out_specs=(vmem, vmem),
         scratch_shapes=[
+            pltpu.VMEM(main_shape, f32),
+            pltpu.VMEM(edge_shape, f32),
+            pltpu.VMEM((1, length), jnp.int32),
+            pltpu.VMEM((length, LANES), f32),
+            pltpu.VMEM(table.shape, jnp.bfloat16),
             pltpu.VMEM((MAXN, TILE, rows), f32),
             pltpu.VMEM((MAXN, TILE, rows), f32),
             pltpu.VMEM((MAXN, TILE, rows), f32),
             pltpu.VMEM((MAXN, TILE, rows), f32),
             pltpu.VMEM((length + TILE, rows), f32),
             pltpu.VMEM((length + TILE, rows), f32),
-            pltpu.VMEM((length + LANES, LANES), f32),
+            pltpu.VMEM((length + TILE, LANES), f32),
             pltpu.VMEM((rows, LANES), f32),
             pltpu.VMEM((rows, LANES), f32),
+            pltpu.SemaphoreType.DMA,
+            pltpu.SemaphoreType.DMA((2,)),
+            pltpu.SemaphoreType.DMA((shape.halves, slabs)),
+            pltpu.SemaphoreType.DMA((shape.halves, slabs)),
+            pltpu.SemaphoreType.DMA((slabs,)),
+            pltpu.SemaphoreType.DMA((slabs,)),
         ],
-        compiler_params=pltpu.CompilerParams(vmem_limit_bytes=48 * 2**20),
-    )(t_start, log_order, counts[None, :], jnp.asarray(fourier_table(rows)))
-    main = lax.all_to_all(main, "res", split_axis=1, concat_axis=1, tiled=True)
-    edge = lax.all_to_all(edge, "res", split_axis=0, concat_axis=0, tiled=True)
+        compiler_params=pltpu.CompilerParams(
+            collective_id=0, has_side_effects=True, vmem_limit_bytes=48 * 2**20
+        ),
+    )(t_start, log_order, term_counts[None, :], jnp.asarray(table))
     return refine_call(shape, main, edge)
 
 

time: 72.4 us -> 46.2 us (0.64)
  blocking collectives: 33.1 us -> 0 us
  Pallas kernels: 23.8 us -> 42.4 us
  waiting for transfers between devices: 6.87 us -> 0 us
  starting transfers between devices: 4.09 us -> 0 us
  other arithmetic: 0.83 us -> 0 us
    all_to_all x1 -> x0, blocking collectives: 33.1 us -> none  [fast_device(): main = lax.all_to_all(main, 'res', split_axis=1, concat_axis=1, tiled=True)]
    pallas_call x1, Pallas kernels: 20.3 us -> 38.9 us  [fast_device(): pl.pallas_call(functools.partial(zeta_kernel, shape), out_shape=(jax.Shap...]
    all_to_all x1 -> x0, waiting for transfers between devices: 6.58 us -> none  [fast_device(): edge = lax.all_to_all(edge, 'res', split_axis=0, concat_axis=0, tiled=True)]
    all_to_all x1 -> x0, starting transfers between devices: 3.64 us -> none  [fast_device(): edge = lax.all_to_all(edge, 'res', split_axis=0, concat_axis=0, tiled=True)]
    select_n x1 -> x0, other arithmetic: 0.83 us -> none  [fast_device(): jnp.where(ta_index == 0, jnp.concatenate([term_counts, other[:TILE], pad]...]
    unnamed x8 -> x10, local copies, waits for them, and re-layouts: 2.29 us -> 2.95 us
  transfers between devices with their start and end apart: 2 -> 0, of which waited for: 2 -> 0; matrix products, arithmetic and copies ran while one was open for 0% -> 0% of each run, Pallas kernels for 0% -> 0%
where the time goes in v2:
time: 46.2 us; the launch traced here: 46.1 us
  Pallas kernels  42.4 us (92%)
  local copies, waits for them, and re-layouts  2.95 us (6%)
  between operations  0.69 us (1%)
    pallas_call x1, Pallas kernels, fast_device(): pl.pallas_call(functools.partial(zeta_kernel, shape), out_shape=(jax.Shap...  38.9 us
    pallas_call x1, Pallas kernels, refine_call(): pl.pallas_call(functools.partial(refine_kernel, shape, chunk), grid=(shap...  3.51 us
    unnamed x10, local copies, waits for them, and re-layouts  2.95 us

profile of v2, /device:TPU:0, one launch (start us, length us, event | category | flops | bytes accessed | tf_op | source)
XLA Modules:
  0.0 46.1 jit_solution(13881423119923264005)
XLA Ops:
  0.7 0.0 copy-start
  0.7 1.6 %copy-done = bf16[4,512,512]{2,1,0:T(8,128)(2,1)S(1)} copy-done((bf16[4,512,512]{2,1,0:T(8,128)(2,1)S(1)}, bf16[4,512,512]{2,1,0:T(8,128)(2,1)}, u32[]{:S(2)}) %copy-start) | copy-done | bytes 2097176
  2.2 0.0 copy-start.3
  2.2 0.7 %copy-done.3 = s32[1,512]{1,0:T(1,128)S(1)} copy-done((s32[1,512]{1,0:T(1,128)S(1)}, s32[1,512]{1,0:T(1,128)}, u32[]{:S(2)}) %copy-start.3) | copy-done | bytes 2072
  2.9 0.0 copy-start.4
  2.9 0.7 %copy-done.4 = s32[256]{0:T(256)S(1)} copy-done((s32[256]{0:T(256)S(1)}, s32[256]{0:T(256)}, u32[]{:S(2)}) %copy-start.4) | copy-done | bytes 1048
  3.6 0.0 copy-start.1
  3.6 0.0 copy-start.2
  3.6 38.9 %shard_map.64 = (f32[2,8,2,64,128]{4,3,2,1,0:T(8,128)S(1)}, f32[8,8,128]{2,1,0:T(8,128)S(1)}) custom-call(s32[1]{0:T(128)S(6)} %copy.7.start_ref, s32[1,512]{1,0:T(1,128)S(1)} %copy-done.3, s32[1,256]{1,0:T(1,128)S(1)} %bitcast.1, bf16[4,512,512]{2,1,0:T(8,128)(2,1)S(1)} %copy-done), custom_call_target="tpu_custom_call" | custom-call | tf_op jit(solution)/shard_map/pallas_call | solution.py:410
  42.5 0.0 copy-done.1
  42.5 0.0 copy-done.2
  42.5 3.5 %shard_map.65 = f32[2,8,64,512]{3,2,1,0:T(8,128)} custom-call(f32[2,8,2,64,128]{4,3,2,1,0:T(8,128)S(1)} %get-tuple-element.7.main_ref, f32[8,8,128]{2,1,0:T(8,128)S(1)} %get-tuple-element.8.edge_ref, bf16[2,256,512]{2,1,0:T(8,128)(2,1)S(1)} %copy-done.2, bf16[2,2,64,1024]{3,2,1,0:T(8,128)(2,1)S(1)} %copy-done.1), custom_call_target="tpu_custom_call" | custom-call | tf_op jit(solution)/shard_map/pallas_call | solution.py:448
Async XLA Ops:
  0.7 1.6 %copy-start = (bf16[4,512,512]{2,1,0:T(8,128)(2,1)S(1)}, bf16[4,512,512]{2,1,0:T(8,128)(2,1)}, u32[]{:S(2)}) copy-start(bf16[4,512,512]{2,1,0:T(8,128)(2,1)} %constant.6.clone.table_hbm) | copy-start | bytes 6291460
  2.2 0.7 %copy-start.3 = (s32[1,512]{1,0:T(1,128)S(1)}, s32[1,512]{1,0:T(1,128)}, u32[]{:S(2)}) copy-start(s32[1,512]{1,0:T(1,128)} %order_ref.1) | copy-start | bytes 6148
  2.9 0.7 %copy-start.4 = (s32[256]{0:T(256)S(1)}, s32[256]{0:T(256)}, u32[]{:S(2)}) copy-start(s32[256]{0:T(256)} %param.8) | copy-start | bytes 3076
  3.6 38.9 %copy-start.1 = (bf16[2,2,64,1024]{3,2,1,0:T(8,128)(2,1)S(1)}, bf16[2,2,64,1024]{3,2,1,0:T(8,128)(2,1)}, u32[]{:S(2)}) copy-start(bf16[2,2,64,1024]{3,2,1,0:T(8,128)(2,1)} %constant.8.clone.edge_tab) | copy-start | bytes 1572868
  3.6 38.9 %copy-start.2 = (bf16[2,256,512]{2,1,0:T(8,128)(2,1)S(1)}, bf16[2,256,512]{2,1,0:T(8,128)(2,1)}, u32[]{:S(2)}) copy-start(bf16[2,256,512]{2,1,0:T(8,128)(2,1)} %constant.7.clone.table) | copy-start | bytes 1572868

commit v3 on v2

--- a/solution.py
+++ b/solution.py
@@ -12,7 +12,12 @@
 
 TAPS = 8
 MAXN = 32
+NMIN = 4
 LANES = 128
+HALF = LANES // 2
+PEER_ORDER = (6, 7, 4, 5, 2, 3, 1)
+NEAR_ORDER = (2, 3, 1)
+TWICE = 2
 TILE = 8
 
 SIN_COEFS = (
@@ -111,6 +116,7 @@
         self.block = rows // slabs
         self.tiles = length // TILE + 1
         self.halves = length // LANES
+        self.chunks = length // HALF
 
 
 def prepare(shape, order_ref, turn_re, turn_im, wave_re, wave_im, base_t):
@@ -141,27 +147,37 @@
         lanes = pl.ds(pl.multiple_of(block * LANES, LANES), LANES)
         limits = [counts[row0 + a * TILE : row0 + (a + 1) * TILE, :] for a in range(count)]
 
-        def term(n, sums):
+        def term(n, sums, masked):
             now_re = wave_re[n, :, lanes]
             now_im = wave_im[n, :, lanes]
             rot_re = turn_re[n, :, lanes]
             rot_im = turn_im[n, :, lanes]
-            n_float = lax.convert_element_type(n, jnp.float32)
+            twice_cos = rot_re + rot_re
+            last_re = last_im = None
             out = []
             for a in range(count):
-                active = limits[a] > n_float
-                out.append(sums[2 * a] + jnp.where(active, now_re, 0.0))
-                out.append(sums[2 * a + 1] + jnp.where(active, now_im, 0.0))
-                now_re, now_im = (
-                    now_re * rot_re - now_im * rot_im,
-                    now_re * rot_im + now_im * rot_re,
-                )
+                if masked:
+                    active = limits[a] > lax.convert_element_type(n, jnp.float32)
+                    out.append(sums[2 * a] + jnp.where(active, now_re, 0.0))
+                    out.append(sums[2 * a + 1] + jnp.where(active, now_im, 0.0))
+                else:
+                    out.append(sums[2 * a] + now_re)
+                    out.append(sums[2 * a + 1] + now_im)
+                if a == 0:
+                    next_re = now_re * rot_re - now_im * rot_im
+                    next_im = now_re * rot_im + now_im * rot_re
+                else:
+                    next_re = twice_cos * now_re - last_re
+                    next_im = twice_cos * now_im - last_im
+                last_re, last_im, now_re, now_im = now_re, now_im, next_re, next_im
             wave_re[n, :, lanes] = now_re
             wave_im[n, :, lanes] = now_im
             return tuple(out)
 
-        zero = jnp.zeros((TILE, LANES), jnp.float32)
-        sums = lax.fori_loop(0, MAXN, term, (zero,) * (2 * count), unroll=4)
+        sums = (jnp.zeros((TILE, LANES), jnp.float32),) * (2 * count)
+        for n in range(NMIN):
+            sums = term(n, sums, False)
+        sums = lax.fori_loop(NMIN, MAXN, functools.partial(term, masked=True), sums, unroll=4)
         residue = jnp.broadcast_to(order_ref[:, lanes].astype(jnp.float32), (TILE, LANES))
         fraction = residue * (1.0 / modulus)
         offsets = lax.broadcasted_iota(jnp.int32, (TILE, LANES), 0).astype(jnp.float32)
@@ -200,27 +216,24 @@
     twist_sin[...] = sin
 
 
-def transform_half(shape, half, skip, zeta_re, zeta_im, tables, twist_cos, twist_sin, store):
-    place = pl.ds(pl.multiple_of(half * LANES + skip, TILE), LANES)
-    both = jnp.concatenate([zeta_re[place, :], zeta_im[place, :]], axis=0)
-    high, low = split_bf16(both)
-    chunk = 2 * shape.block
-    for piece in range(shape.rows // chunk):
-        rows = slice(piece * chunk, (piece + 1) * chunk)
-        cos_high = tables[0, rows, :]
-        sin_high = tables[2, rows, :]
-        with_cos = dot_nt(cos_high, high) + dot_nt(cos_high, low) + dot_nt(tables[1, rows, :], high)
-        with_sin = dot_nt(sin_high, high) + dot_nt(sin_high, low) + dot_nt(tables[3, rows, :], high)
-        mixed_re = with_cos[:, :LANES] - with_sin[:, LANES:]
-        mixed_im = with_sin[:, :LANES] + with_cos[:, LANES:]
-        t_cos = twist_cos[rows, :]
-        t_sin = twist_sin[rows, :]
-        out_re = t_cos * mixed_re - t_sin * mixed_im
-        out_im = t_sin * mixed_re + t_cos * mixed_im
+def transform_chunk(shape, chunk, skip, first_block, blocks, zeta_re, zeta_im, tables, twist_cos, twist_sin, store):
+    place = pl.ds(pl.multiple_of(chunk * HALF + skip, TILE), HALF)
+    high, low = split_bf16(jnp.concatenate([zeta_re[place, :], zeta_im[place, :]], axis=0))
+    both = jnp.concatenate([high, low], axis=0)
+    cut_rows = 2 * shape.block
+    lane = lax.broadcasted_iota(jnp.int32, (cut_rows, LANES), 1)
+    sign = jnp.where(lane < HALF, -1.0, 1.0)
+    for piece in range(blocks // 2):
+        start = first_block * shape.block + piece * cut_rows
+        rows = pl.ds(pl.multiple_of(start, cut_rows), cut_rows)
+        with_cos = dot_nt(tables[0, rows, :], both)
+        with_sin = dot_nt(tables[2, rows, :], both)
+        with_cos = with_cos[:, :LANES] + with_cos[:, LANES:] + dot_nt(tables[1, rows, :], high)
+        with_sin = with_sin[:, :LANES] + with_sin[:, LANES:] + dot_nt(tables[3, rows, :], high)
+        mixed = with_cos + sign * pltpu.roll(with_sin, HALF, 1)
+        out = twist_cos[rows, :] * mixed + (sign * twist_sin[rows, :]) * pltpu.roll(mixed, HALF, 1)
         for sub in range(2):
-            cut = slice(sub * shape.block, (sub + 1) * shape.block)
-            store(2 * piece + sub, 0, out_re[cut])
-            store(2 * piece + sub, 1, out_im[cut])
+            store(2 * piece + sub, out[sub * shape.block : (sub + 1) * shape.block])
 
 
 def transform_edge(shape, place, slab_index, zeta_re, zeta_im, tables, store):
@@ -262,15 +275,22 @@
     ]
 
 
+def flipped(index, bits):
+    for bit in (1, 2, 4):
+        if bits & bit:
+            index = index + bit * (1 - 2 * ((index // bit) % 2))
+    return index
+
+
 def zeta_kernel(shape, start_ref, order_ref, count_ref, table_hbm, main_out, edge_out, main_send, edge_send,
-                other_counts, spare, tables, turn_re, turn_im, wave_re, wave_im, zeta_re, zeta_im, counts,
+                other_counts, other_order, spare, tables, turn_re, turn_im, wave_re, wave_im, zeta_re, zeta_im, counts,
                 twist_cos, twist_sin, table_sem, count_sems, main_send_sems, main_recv_sems,
                 edge_send_sems, edge_recv_sems):
     slabs, length = shape.slabs, shape.length
     me = lax.axis_index("res")
     ta_index = lax.axis_index("ta")
     mesh_ids = pl.DeviceIdType.MESH
-    peers = [lax.rem(me + d, slabs) for d in range(slabs)]
+    peers = [flipped(me, d) for d in range(slabs)]
 
     barrier = pltpu.get_barrier_semaphore()
     for d in range(1, slabs):
@@ -287,8 +307,14 @@
         device_id={"ta": 1 - ta_index}, device_id_type=mesh_ids,
     )
     count_copy.start()
+    order_copy = pltpu.make_async_remote_copy(
+        src_ref=order_ref, dst_ref=other_order, send_sem=count_sems.at[2], recv_sem=count_sems.at[3],
+        device_id={"res": peers[slabs // 2]}, device_id_type=mesh_ids,
+    )
+    order_copy.start()
     prepare(shape, order_ref, turn_re, turn_im, wave_re, wave_im, base_t)
     count_copy.wait()
+    order_copy.wait()
     column_counts(shape, count_ref, other_counts, ta_index * TILE, ta_index * (length - TILE),
                   (1 - ta_index) * length, counts, spare)
 
@@ -302,32 +328,54 @@
         copy.start()
         copies.append(copy)
 
-    first = 0
-    for half in range(shape.halves):
-        for count in ((9, 8) if half == 0 else (8, 8)):
-            sum_tiles(shape, first, count, order_ref, counts, turn_re, turn_im, wave_re, wave_im,
-                      zeta_re, zeta_im, base_t)
-            first += count
-        if half == 0:
+    def sums_and_blocks(order, chunk, extra, first, blocks, store):
+        start = chunk * (HALF // TILE) + (0 if extra else 1)
+        sum_tiles(shape, start, HALF // TILE + extra, order, counts, turn_re, turn_im, wave_re, wave_im,
+                  zeta_re, zeta_im, base_t)
+        if order is order_ref and chunk == 0:
             table_copy.wait()
-
-        def store(block, part, values, half=half):
-            main_send[half, block, part] = values
-
-        transform_half(shape, half, ta_index * TILE, zeta_re, zeta_im, tables, twist_cos, twist_sin, store)
-        for d in range(1, slabs):
-            send(main_send.at[half, peers[d]], main_out.at[half, me],
-                 main_send_sems.at[half, d], main_recv_sems.at[half, d], d)
-        main_out[half, me] = main_send[half, me]
+        transform_chunk(shape, chunk, ta_index * TILE, first, blocks, zeta_re, zeta_im, tables,
+                        twist_cos, twist_sin, store)
+
+    near = slabs // 2
+    near_first = (me // near) * near
+    far_first = near - near_first
+    split = shape.chunks - TWICE
+    for chunk in range(shape.chunks):
+        wide = chunk < split
+        first = 0 if wide else near_first
+
+        def store(block, values, chunk=chunk, first=first):
+            main_send[chunk, first + block] = values
+
+        sums_and_blocks(order_ref, chunk, int(chunk == 0), first, slabs if wide else near, store)
+        for d in PEER_ORDER if wide else NEAR_ORDER:
+            send(main_send.at[chunk, peers[d]], main_out.at[chunk, me],
+                 main_send_sems.at[chunk, d], main_recv_sems.at[chunk, d], d)
+        main_out[chunk, me] = main_send[chunk, me]
 
     def store_edge(block, values):
         edge_send[block] = values
 
     edge_place = pl.ds(pl.multiple_of((1 - ta_index) * length, TILE), TILE)
     transform_edge(shape, edge_place, me, zeta_re, zeta_im, tables, store_edge)
-    for d in range(1, slabs):
+    for d in PEER_ORDER:
         send(edge_send.at[peers[d]], edge_out.at[me], edge_send_sems.at[d], edge_recv_sems.at[d], d)
     edge_out[me] = edge_send[me]
+
+    partner = peers[near]
+    prepare(shape, other_order, turn_re, turn_im, wave_re, wave_im, base_t + float(split * HALF))
+    make_twist(shape, partner, twist_cos, twist_sin)
+    for chunk in range(split, shape.chunks):
+
+        def store(block, values, chunk=chunk):
+            main_send[chunk, far_first + block] = values
+
+        sums_and_blocks(other_order, chunk, int(chunk == split), near_first, near, store)
+        for d in NEAR_ORDER:
+            send(main_send.at[chunk, peers[near + d]], main_out.at[chunk, partner],
+                 main_send_sems.at[chunk, near + d], main_recv_sems.at[chunk, near + d], d)
+        main_out[chunk, partner] = main_send[chunk, partner]
     for copy in copies:
         copy.wait()
 
@@ -379,11 +427,16 @@
         tab_low = edge_tab[ta_index, 1]
         edge_out[...] = dot_nn(high, tab_high) + dot_nn(low, tab_high) + dot_nn(high, tab_low)
 
+    low_half = lax.broadcasted_iota(jnp.int32, (chunk, LANES), 1) < half_lanes
     parts = []
     for p in range(slabs):
-        re = jnp.concatenate([main_ref[h, p, 0] for h in range(shape.halves)], axis=1)
-        im = jnp.concatenate([main_ref[h, p, 1] for h in range(shape.halves)], axis=1)
-        parts.append((re, im))
+        re, im = [], []
+        for h in range(shape.halves):
+            left = main_ref[2 * h, p]
+            right = main_ref[2 * h + 1, p]
+            re.append(jnp.where(low_half, left, pltpu.roll(right, half_lanes, 1)))
+            im.append(jnp.where(low_half, pltpu.roll(left, half_lanes, 1), right))
+        parts.append((jnp.concatenate(re, axis=1), jnp.concatenate(im, axis=1)))
     mixed = fft_eight(parts)
     stacked = jnp.concatenate([m[0] for m in mixed] + [m[1] for m in mixed], axis=0)
     high, low = split_bf16(stacked)
@@ -404,7 +457,7 @@
     rows, slabs, length = shape.rows, shape.slabs, shape.length
     f32 = jnp.float32
     vmem = pl.BlockSpec(memory_space=pltpu.VMEM)
-    main_shape = (shape.halves, slabs, 2, shape.block, LANES)
+    main_shape = (shape.chunks, slabs, shape.block, LANES)
     edge_shape = (slabs, TILE, LANES)
     table = fourier_table(rows)
     main, edge = pl.pallas_call(
@@ -416,6 +469,7 @@
             pltpu.VMEM(main_shape, f32),
             pltpu.VMEM(edge_shape, f32),
             pltpu.VMEM((1, length), jnp.int32),
+            pltpu.VMEM((1, rows), jnp.int32),
             pltpu.VMEM((length, LANES), f32),
             pltpu.VMEM(table.shape, jnp.bfloat16),
             pltpu.VMEM((MAXN, TILE, rows), f32),
@@ -428,9 +482,9 @@
             pltpu.VMEM((rows, LANES), f32),
             pltpu.VMEM((rows, LANES), f32),
             pltpu.SemaphoreType.DMA,
-            pltpu.SemaphoreType.DMA((2,)),
-            pltpu.SemaphoreType.DMA((shape.halves, slabs)),
-            pltpu.SemaphoreType.DMA((shape.halves, slabs)),
+            pltpu.SemaphoreType.DMA((4,)),
+            pltpu.SemaphoreType.DMA((shape.chunks, slabs)),
+            pltpu.SemaphoreType.DMA((shape.chunks, slabs)),
             pltpu.SemaphoreType.DMA((slabs,)),
             pltpu.SemaphoreType.DMA((slabs,)),
         ],
@@ -450,7 +504,7 @@
         grid=(shape.block // chunk,),
         out_shape=jax.ShapeDtypeStruct((2, slabs, shape.block, 2 * length), f32),
         in_specs=[
-            pl.BlockSpec((shape.halves, slabs, 2, chunk, LANES), lambda i: (0, 0, 0, i, 0)),
+            pl.BlockSpec((shape.chunks, slabs, chunk, LANES), lambda i: (0, 0, i, 0)),
             pl.BlockSpec((slabs, TILE, LANES), lambda i: (0, 0, 0)),
             pl.BlockSpec((2, length, 2 * length), lambda i: (0, 0, 0)),
             pl.BlockSpec((2, 2, slabs * TILE, slabs * LANES), lambda i: (0, 0, 0, 0)),

time: 46.2 us -> 38.6 us (0.84)
  Pallas kernels: 42.4 us -> 34.8 us
    pallas_call x1, Pallas kernels: 38.9 us -> 30.9 us  [fast_device(): pl.pallas_call(functools.partial(zeta_kernel, shape), out_shape=(jax.Shap...]
where the time goes in v3:
time: 38.6 us; the launch traced here: 38.4 us
  Pallas kernels  34.8 us (90%)
  local copies, waits for them, and re-layouts  2.95 us (8%)
  between operations  0.69 us (2%)
    pallas_call x1, Pallas kernels, fast_device(): pl.pallas_call(functools.partial(zeta_kernel, shape), out_shape=(jax.Shap...  30.9 us
    pallas_call x1, Pallas kernels, refine_call(): pl.pallas_call(functools.partial(refine_kernel, shape, chunk), grid=(shap...  3.83 us
    unnamed x10, local copies, waits for them, and re-layouts  2.95 us

profile of v3, /device:TPU:0, one launch (start us, length us, event | category | flops | bytes accessed | tf_op | source)
XLA Modules:
  0.0 38.4 jit_solution(5087830482473322528)
XLA Ops:
  0.7 0.0 copy-start
  0.7 1.6 %copy-done = bf16[4,512,512]{2,1,0:T(8,128)(2,1)S(1)} copy-done((bf16[4,512,512]{2,1,0:T(8,128)(2,1)S(1)}, bf16[4,512,512]{2,1,0:T(8,128)(2,1)}, u32[]{:S(2)}) %copy-start) | copy-done | bytes 2097176
  2.2 0.0 copy-start.3
  2.2 0.7 %copy-done.3 = s32[1,512]{1,0:T(1,128)S(1)} copy-done((s32[1,512]{1,0:T(1,128)S(1)}, s32[1,512]{1,0:T(1,128)}, u32[]{:S(2)}) %copy-start.3) | copy-done | bytes 2072
  2.9 0.0 copy-start.4
  2.9 0.7 %copy-done.4 = s32[256]{0:T(256)S(1)} copy-done((s32[256]{0:T(256)S(1)}, s32[256]{0:T(256)}, u32[]{:S(2)}) %copy-start.4) | copy-done | bytes 1048
  3.6 0.0 copy-start.1
  3.6 0.0 copy-start.2
  3.6 30.9 %shard_map.64 = (f32[4,8,64,128]{3,2,1,0:T(8,128)S(1)}, f32[8,8,128]{2,1,0:T(8,128)S(1)}) custom-call(s32[1]{0:T(128)S(6)} %copy.7.start_ref, s32[1,512]{1,0:T(1,128)S(1)} %copy-done.3, s32[1,256]{1,0:T(1,128)S(1)} %bitcast.1, bf16[4,512,512]{2,1,0:T(8,128)(2,1)S(1)} %copy-done), custom_call_target="tpu_custom_call" | custom-call | tf_op jit(solution)/shard_map/pallas_call | solution.py:463
  34.6 0.0 copy-done.1
  34.6 0.0 copy-done.2
  34.6 3.8 %shard_map.65 = f32[2,8,64,512]{3,2,1,0:T(8,128)} custom-call(f32[4,8,64,128]{3,2,1,0:T(8,128)S(1)} %get-tuple-element.7.main_ref, f32[8,8,128]{2,1,0:T(8,128)S(1)} %get-tuple-element.8.edge_ref, bf16[2,256,512]{2,1,0:T(8,128)(2,1)S(1)} %copy-done.2, bf16[2,2,64,1024]{3,2,1,0:T(8,128)(2,1)S(1)} %copy-done.1), custom_call_target="tpu_custom_call" | custom-call | tf_op jit(solution)/shard_map/pallas_call | solution.py:502
Async XLA Ops:
  0.7 1.6 %copy-start = (bf16[4,512,512]{2,1,0:T(8,128)(2,1)S(1)}, bf16[4,512,512]{2,1,0:T(8,128)(2,1)}, u32[]{:S(2)}) copy-start(bf16[4,512,512]{2,1,0:T(8,128)(2,1)} %constant.6.clone.table_hbm) | copy-start | bytes 6291460
  2.2 0.7 %copy-start.3 = (s32[1,512]{1,0:T(1,128)S(1)}, s32[1,512]{1,0:T(1,128)}, u32[]{:S(2)}) copy-start(s32[1,512]{1,0:T(1,128)} %order_ref.1) | copy-start | bytes 6148
  2.9 0.7 %copy-start.4 = (s32[256]{0:T(256)S(1)}, s32[256]{0:T(256)}, u32[]{:S(2)}) copy-start(s32[256]{0:T(256)} %param.8) | copy-start | bytes 3076
  3.6 30.9 %copy-start.1 = (bf16[2,2,64,1024]{3,2,1,0:T(8,128)(2,1)S(1)}, bf16[2,2,64,1024]{3,2,1,0:T(8,128)(2,1)}, u32[]{:S(2)}) copy-start(bf16[2,2,64,1024]{3,2,1,0:T(8,128)(2,1)} %constant.8.clone.edge_tab) | copy-start | bytes 1572868
  3.6 31.0 %copy-start.2 = (bf16[2,256,512]{2,1,0:T(8,128)(2,1)S(1)}, bf16[2,256,512]{2,1,0:T(8,128)(2,1)}, u32[]{:S(2)}) copy-start(bf16[2,256,512]{2,1,0:T(8,128)(2,1)} %constant.7.clone.table) | copy-start | bytes 1572868

commit v4 on v3

--- a/solution.py
+++ b/solution.py
@@ -142,6 +142,12 @@
 def sum_tiles(shape, first, count, order_ref, counts, turn_re, turn_im, wave_re, wave_im, zeta_re, zeta_im, base_t):
     modulus = float(shape.slabs * shape.rows + 1)
     row0 = first * TILE
+    offsets = lax.broadcasted_iota(jnp.int32, (TILE, LANES), 0).astype(jnp.float32)
+    per_tile = []
+    for a in range(count):
+        t_now = (base_t + float(row0 + a * TILE) + offsets) * 0.0625
+        t_square = t_now * t_now
+        per_tile.append((t_now, 1.0 / (0.25 + t_square), 1.875 - 4.5 * t_square, t_now * (5.75 - t_square)))
 
     def lane_block(block, carry):
         lanes = pl.ds(pl.multiple_of(block * LANES, LANES), LANES)
@@ -180,14 +186,9 @@
         sums = lax.fori_loop(NMIN, MAXN, functools.partial(term, masked=True), sums, unroll=4)
         residue = jnp.broadcast_to(order_ref[:, lanes].astype(jnp.float32), (TILE, LANES))
         fraction = residue * (1.0 / modulus)
-        offsets = lax.broadcasted_iota(jnp.int32, (TILE, LANES), 0).astype(jnp.float32)
         for a in range(count):
             limit = limits[a]
-            t_now = (base_t + float(row0 + a * TILE) + offsets) * 0.0625
-            t_square = t_now * t_now
-            inverse_den = 1.0 / (0.25 + t_square)
-            cubic_re = 1.875 - 4.5 * t_square
-            cubic_im = t_now * (5.75 - t_square)
+            t_now, inverse_den, cubic_re, cubic_im = per_tile[a]
             whole_base = limit * modulus + residue
             tail_base = limit + fraction
             inverse = 1.0 / tail_base

time: 38.6 us -> 38.6 us (level)
  no operation moved by 1% of the time
where the time goes in v4:
time: 38.6 us; the launch traced here: 38.4 us
  Pallas kernels  34.8 us (90%)
  local copies, waits for them, and re-layouts  2.95 us (8%)
  between operations  0.69 us (2%)
    pallas_call x1, Pallas kernels, fast_device(): pl.pallas_call(functools.partial(zeta_kernel, shape), out_shape=(jax.Shap...  30.9 us
    pallas_call x1, Pallas kernels, refine_call(): pl.pallas_call(functools.partial(refine_kernel, shape, chunk), grid=(shap...  3.83 us
    unnamed x10, local copies, waits for them, and re-layouts  2.95 us

profile of v4, /device:TPU:0, one launch (start us, length us, event | category | flops | bytes accessed | tf_op | source)
XLA Modules:
  0.0 38.4 jit_solution(11894845621773048106)
XLA Ops:
  0.7 0.0 copy-start
  0.7 1.6 %copy-done = bf16[4,512,512]{2,1,0:T(8,128)(2,1)S(1)} copy-done((bf16[4,512,512]{2,1,0:T(8,128)(2,1)S(1)}, bf16[4,512,512]{2,1,0:T(8,128)(2,1)}, u32[]{:S(2)}) %copy-start) | copy-done | bytes 2097176
  2.2 0.0 copy-start.3
  2.2 0.7 %copy-done.3 = s32[1,512]{1,0:T(1,128)S(1)} copy-done((s32[1,512]{1,0:T(1,128)S(1)}, s32[1,512]{1,0:T(1,128)}, u32[]{:S(2)}) %copy-start.3) | copy-done | bytes 2072
  2.9 0.0 copy-start.4
  2.9 0.7 %copy-done.4 = s32[256]{0:T(256)S(1)} copy-done((s32[256]{0:T(256)S(1)}, s32[256]{0:T(256)}, u32[]{:S(2)}) %copy-start.4) | copy-done | bytes 1048
  3.6 0.0 copy-start.1
  3.6 0.0 copy-start.2
  3.6 30.9 %shard_map.64 = (f32[4,8,64,128]{3,2,1,0:T(8,128)S(1)}, f32[8,8,128]{2,1,0:T(8,128)S(1)}) custom-call(s32[1]{0:T(128)S(6)} %copy.7.start_ref, s32[1,512]{1,0:T(1,128)S(1)} %copy-done.3, s32[1,256]{1,0:T(1,128)S(1)} %bitcast.1, bf16[4,512,512]{2,1,0:T(8,128)(2,1)S(1)} %copy-done), custom_call_target="tpu_custom_call" | custom-call | tf_op jit(solution)/shard_map/pallas_call | solution.py:464
  34.5 0.0 copy-done.1
  34.6 0.0 copy-done.2
  34.6 3.8 %shard_map.65 = f32[2,8,64,512]{3,2,1,0:T(8,128)} custom-call(f32[4,8,64,128]{3,2,1,0:T(8,128)S(1)} %get-tuple-element.7.main_ref, f32[8,8,128]{2,1,0:T(8,128)S(1)} %get-tuple-element.8.edge_ref, bf16[2,256,512]{2,1,0:T(8,128)(2,1)S(1)} %copy-done.2, bf16[2,2,64,1024]{3,2,1,0:T(8,128)(2,1)S(1)} %copy-done.1), custom_call_target="tpu_custom_call" | custom-call | tf_op jit(solution)/shard_map/pallas_call | solution.py:503
Async XLA Ops:
  0.7 1.6 %copy-start = (bf16[4,512,512]{2,1,0:T(8,128)(2,1)S(1)}, bf16[4,512,512]{2,1,0:T(8,128)(2,1)}, u32[]{:S(2)}) copy-start(bf16[4,512,512]{2,1,0:T(8,128)(2,1)} %constant.6.clone.table_hbm) | copy-start | bytes 6291460
  2.2 0.7 %copy-start.3 = (s32[1,512]{1,0:T(1,128)S(1)}, s32[1,512]{1,0:T(1,128)}, u32[]{:S(2)}) copy-start(s32[1,512]{1,0:T(1,128)} %order_ref.1) | copy-start | bytes 6148
  2.9 0.7 %copy-start.4 = (s32[256]{0:T(256)S(1)}, s32[256]{0:T(256)}, u32[]{:S(2)}) copy-start(s32[256]{0:T(256)} %param.8) | copy-start | bytes 3076
  3.6 30.9 %copy-start.1 = (bf16[2,2,64,1024]{3,2,1,0:T(8,128)(2,1)S(1)}, bf16[2,2,64,1024]{3,2,1,0:T(8,128)(2,1)}, u32[]{:S(2)}) copy-start(bf16[2,2,64,1024]{3,2,1,0:T(8,128)(2,1)} %constant.8.clone.edge_tab) | copy-start | bytes 1572868
  3.6 30.9 %copy-start.2 = (bf16[2,256,512]{2,1,0:T(8,128)(2,1)S(1)}, bf16[2,256,512]{2,1,0:T(8,128)(2,1)}, u32[]{:S(2)}) copy-start(bf16[2,256,512]{2,1,0:T(8,128)(2,1)} %constant.7.clone.table) | copy-start | bytes 1572868
